TPU v7x, 128 devices: a whole 4x4x4 slice. The times are simulated.
128 devices in a mesh: ctx: 16 (over x, y_hi, core), head: 8 (over y_lo, z).
Axes of the slice: x: 4, y: 4 (y_hi: 2, y_lo: 2; y = y_hi * 2 + y_lo), z: 4, core: 2. Of those that a mesh axis runs over, the one named last changes fastest.
Arguments:
- queries: bfloat16 [8192, 8192], P('ctx', 'head'), may hold values from -100 to 100
- key_states: bfloat16 [8192, 1024], P('ctx', 'head'), may hold values from -4.5 to 4.5
- value_states: bfloat16 [8192, 1024], P('ctx', 'head'), may hold values from -6 to 6
- doc_ids: int32 [8192], P('ctx'), may hold values from 0 to 7, never falling along the last dimension, each value on 1 to 4096 neighbouring positions
- out_weight: bfloat16 [8192, 4096], P('head'), may hold values from -0.0625 to 0.0625
Outputs:
- projected: bfloat16 [8192, 4096], P(('ctx', 'head'))
Inputs may be any that keep to these rules, and one draw needn't show every extreme that they name: `doc_ids`: never falling along the sequence; each document has 1 to 4096 tokens, one exactly 4096.
All inputs are finite; a program needn't handle non-finite values.
Results may differ from a plain program's by a relative error of at most 0.018.
Values may be sent and summed in bfloat16 or wider, within the bound.
A program may use at most 64 MiB of HBM per device.

v0:
```python
import jax
import jax.numpy as jnp
from jax import lax
from jax.sharding import PartitionSpec as P

DH = 128


def on_device(queries, key_states, value_states, doc_ids, out_weight):
    tok_rows = queries.shape[0]
    half_rows = tok_rows // 2
    kv_groups = key_states.shape[1] // DH
    per_group = queries.shape[1] // key_states.shape[1]
    my_index = lax.axis_index("ctx")
    attn_scale = DH ** (-0.5)
    work_pos = my_index * tok_rows + jnp.arange(tok_rows, dtype=jnp.int32)
    shaped_q = queries.reshape(tok_rows, kv_groups, per_group, DH)
    q_parts = []
    for q_part in range(2):
        lower = q_part * half_rows
        q_parts.append(
            (
                shaped_q[lower : lower + half_rows],
                work_pos[lower : lower + half_rows],
                doc_ids[lower : lower + half_rows],
            )
        )

    def update(q_state, key_blk, value_blk, key_pos, key_doc, query_blk, query_pos, query_doc):
        top_score, denom_sum, weighted = q_state
        scores = (
            jnp.einsum("qghd,kgd->ghqk", query_blk, key_blk, preferred_element_type=jnp.float32)
            * attn_scale
        )
        allowed = (key_pos[None, :] <= query_pos[:, None]) & (
            key_doc[None, :] == query_doc[:, None]
        )
        masked = jnp.where(allowed[None, None], scores, -1e30)
        new_top = jnp.maximum(top_score, jnp.max(masked, axis=-1))
        prob_rows = jnp.where(allowed[None, None], jnp.exp(masked - new_top[..., None]), 0.0)
        rescale = jnp.exp(top_score - new_top)
        denom_sum = denom_sum * rescale + jnp.sum(prob_rows, axis=-1)
        weighted = weighted * rescale[..., None] + jnp.einsum(
            "ghqk,kgd->ghqd",
            prob_rows.astype(jnp.bfloat16),
            value_blk,
            preferred_element_type=jnp.float32,
        )
        return (new_top, denom_sum, weighted)

    def fresh_state():
        return (
            jnp.full((kv_groups, per_group, half_rows), -1e30, jnp.float32),
            jnp.zeros((kv_groups, per_group, half_rows), jnp.float32),
            jnp.zeros((kv_groups, per_group, half_rows, DH), jnp.float32),
        )

    key_rows = lax.all_gather(key_states, "ctx", axis=0, tiled=True)
    value_rows = lax.all_gather(value_states, "ctx", axis=0, tiled=True)
    key_ids = lax.all_gather(doc_ids, "ctx", axis=0, tiled=True)
    key_count = key_rows.shape[0]
    key_block = 512
    num_blocks = key_count // key_block
    blocked = (
        key_rows.reshape(num_blocks, key_block, kv_groups, DH),
        value_rows.reshape(num_blocks, key_block, kv_groups, DH),
        jnp.arange(key_count, dtype=jnp.int32).reshape(num_blocks, key_block),
        key_ids.reshape(num_blocks, key_block),
    )

    def step_block(states, block_data):
        key_blk, value_blk, key_pos, key_doc = block_data
        next_states = []
        for q_part in range(2):
            query_blk, query_pos, query_doc = q_parts[q_part]
            is_live = (
                (key_pos[0] <= query_pos[-1])
                & (jnp.min(key_doc) <= jnp.max(query_doc))
                & (jnp.max(key_doc) >= jnp.min(query_doc))
            )
            next_states.append(
                lax.cond(
                    is_live,
                    lambda q_state: update(
                        q_state,
                        key_blk,
                        value_blk,
                        key_pos,
                        key_doc,
                        query_blk,
                        query_pos,
                        query_doc,
                    ),
                    lambda q_state: q_state,
                    states[q_part],
                )
            )
        return (tuple(next_states), None)

    result, unused = lax.scan(step_block, (fresh_state(), fresh_state()), blocked)
    outputs = [q_state[2] / q_state[1][..., None] for q_state in result]
    combined = jnp.concatenate(outputs, axis=2)
    attended = (
        jnp.transpose(combined, (2, 0, 1, 3))
        .reshape(tok_rows, kv_groups * per_group * DH)
        .astype(jnp.bfloat16)
    )
    return lax.psum_scatter(
        jnp.dot(attended, out_weight, preferred_element_type=jnp.float32).astype(jnp.bfloat16),
        "head",
        scatter_dimension=0,
        tiled=True,
    )


def solution(mesh):
    return jax.shard_map(
        on_device,
        mesh=mesh,
        in_specs=(P("ctx", "head"), P("ctx", "head"), P("ctx", "head"), P("ctx"), P("head", None)),
        out_specs=P(("ctx", "head"), None),
        check_vma=False,
    )
```

profile of v0, /device:TPU:1, one launch (start us, length us, event | category | flops | bytes accessed | tf_op | source)
XLA Modules:
  0.0 416.2 jit_solution(7356006265081417582)
XLA Ops:
  8.1 1.3 fusion.43
  10.3 25.7 %all-gather = s32[16,1,512]{2,1,0:T(1,128)S(1)} all-gather(s32[1,1,512]{2,1,0:T(1,128)S(1)} %bitcast.158), channel_id=1, replica_groups=mesh['ctx'=16,'head'=8] {'ctx'}, dimensions={0}, use_global_device_ids=true | all-gather | bytes 34816 | tf_op jit(solution)/shard_map/all_gather | solution.py:60
  36.8 25.0 %all-gather.4.cloned.1.call-done = bf16[8192,128]{1,0:T(8,128)(2,1)} async-done(((bf16[512,128]{1,0:T(8,128)(2,1)}), bf16[8192,128]{1,0:T(8,128)(2,1)}) %all-gather.4.cloned.1.call-update) | async-done | bytes 2097168 | tf_op jit(solution)/shard_map/all_gather | solution.py:58
  61.8 49.6 %all-gather.6.cloned.1.call-done = bf16[8192,128]{1,0:T(8,128)(2,1)} async-done(((bf16[512,128]{1,0:T(8,128)(2,1)}), bf16[8192,128]{1,0:T(8,128)(2,1)}) %all-gather.6.cloned.1.call-update) | async-done | bytes 2097168 | tf_op jit(solution)/shard_map/all_gather | solution.py:59
  111.6 189.6 %while.21 = (s32[]{:T(128)}, f32[1,8,256]{2,1,0:T(8,128)S(1)}, f32[1,8,256]{2,1,0:T(8,128)S(1)}, f32[1,8,256,128]{3,2,1,0:T(8,128)S(1)}, f32[1,8,256]{2,1,0:T(8,...) while((s32[]{:T(128)}, f32[1,8,256]{2,1,0:T(8,128)S(1)}, ...), condition=%wide.region_15.16_spmd, body=%wide.region_4.15_spmd.sunk | while | flops 1102853120 | bytes 32789068 | solution.py:100
  112.3 1.0 dynamic-slice_bitcast_fusion.3
  118.1 3.7 conditional.5
  119.2 1.0 fusion.23
  120.2 1.6 fusion.31
  126.2 3.7 conditional.4
  127.2 1.0 fusion.2
  128.3 1.6 fusion.10
  136.4 3.7 conditional.5
  137.4 1.0 fusion.23
  138.5 1.6 fusion.31
  144.5 3.7 conditional.4
  145.5 1.0 fusion.2
  146.5 1.6 fusion.10
  258.1 1.0 dynamic-slice_bitcast_fusion.3
  290.9 1.0 dynamic-slice_bitcast_fusion.3
  301.2 1.3 copy.22
  302.8 1.3 divide_convert_fusion.1
  304.4 9.5 %convolution_convert_fusion = bf16[512,4096]{1,0:T(8,128)(2,1)} fusion(bf16[512,1024]{0,1:T(8,128)(2,1)S(1)} %bitcast.148, bf16[1024,4096]{1,0:T(8,128)(2,1)} %param.15), kind=kOutput, calls=%fused_computation.49 | convolution fusion | flops 4297064448 | bytes 13631488 | tf_op jit(solution)/shard_map/dot_general | solution.py:109
  313.9 95.8 %reduce-scatter.2.cloned.1.call-done = bf16[64,4096]{1,0:T(8,128)(2,1)} async-done(((bf16[512,4096]{1,0:T(8,128)(2,1)}), bf16[64,4096]{1,0:T(8,128)(2,1)}) %reduce-scatter.2.cloned.1.call-update) | async-done | bytes 524304 | tf_op jit(solution)/shard_map/reduce_scatter | solution.py:108
  (150 shorter events, 60.6 us)
Async XLA Ops:
  6.5 3.8 copy-start
  6.5 55.3 %all-gather.4.cloned.1.call-start = ((), (), s32[]{:S(2)}) async-start(), calls=%async_computation.1 | async-start | bytes 2228224 | tf_op jit(solution)/shard_map/all_gather | solution.py:58
  7.3 104.2 %all-gather.6.cloned.1.call-start = ((), (), s32[]{:S(2)}) async-start(), calls=%async_computation.2 | async-start | bytes 2228224 | tf_op jit(solution)/shard_map/all_gather | solution.py:59
  8.0 401.7 %reduce-scatter.2.cloned.1.call-start = ((), (), s32[]{:S(2)}) async-start(), calls=%async_computation.3 | async-start | bytes 4718592 | tf_op jit(solution)/shard_map/reduce_scatter | solution.py:108
Sparse Core Ops, SparseCore 0:
  9.8 51.9 all-gather.3
  64.2 47.1 all-gather.5
  314.0 95.6 reduce-scatter.1
where the time goes:
time: 418 us; the launch traced here: 416 us
  waiting for transfers between devices  172 us (41%)
  loops' own time  120 us (29%)
  local copies, waits for them, and re-layouts  48.4 us (12%)
  blocking collectives  25.7 us (6%)
  matrix products  19 us (5%)
  other arithmetic  18.1 us (4%)
  between operations  13.2 us (3%)
    another operation x1, loops' own time, on_device(): lax.scan(step_block, (fresh_state(), fresh_state()), blocked)  119 us
    reduce_scatter x1, waiting for transfers between devices, on_device(): lax.psum_scatter(jnp.dot(attended, out_weight, preferred_element_type=jnp...  95.8 us
    all_gather x1, waiting for transfers between devices, on_device(): value_rows = lax.all_gather(value_states, 'ctx', axis=0, tiled=True)  49.6 us
    all_gather x1, blocking collectives, on_device(): key_ids = lax.all_gather(doc_ids, 'ctx', axis=0, tiled=True)  25.7 us
    all_gather x1, waiting for transfers between devices, on_device(): key_rows = lax.all_gather(key_states, 'ctx', axis=0, tiled=True)  25 us
    slice x32, local copies, waits for them, and re-layouts, step_block(): query_pos[-1]  19.2 us
    squeeze x16, local copies, waits for them, and re-layouts, on_device(): lax.scan(step_block, (fresh_state(), fresh_state()), blocked)  15.8 us
    reduce_max x16, other arithmetic, step_block(): jnp.max(key_doc) >= jnp.min(query_doc)  10.9 us
  transfers between devices with their start and end apart: 3, of which 3 were waited for; matrix products, arithmetic and copies ran while one was open for 1% of the time, Pallas kernels for 0%

commit v1 on v0

v1 whole, which is shorter than its diff:
```python
import jax
import jax.numpy as jnp
from jax import lax
from jax.experimental import pallas as pl
from jax.experimental.pallas import tpu as pltpu
from jax.sharding import PartitionSpec as P

DH = 128
TOK = 512
VROWS = 144
BLOCK = TOK + 4 * VROWS
SLOTS = 9
UNITS = 16
D_OUT = 4096
PIECES = 4
PCOLS = D_OUT // PIECES
EXP_SCALE = DH**-0.5 * 1.4426950408889634
FAR = -1e30
MESH = pl.DeviceIdType.MESH
NT = (((1,), (1,)), ((), ()))
bf16 = jnp.bfloat16
f32 = jnp.float32


def kernel(
    q_ref, k_ref, v_ref, ids_ref, w_hbm, out_ref,
    kv, kf, qx, s0, s1, mx0, mx1, top, acc, att, w, part, own,
    r_a, r_b, r_up, r_down, y_out, y_in,
    kv_send, kv_recv, rs_send, rs_recv, w_sem,
):
    c = lax.axis_index("ctx")
    h = lax.axis_index("head")
    x = c // 4
    y_hi = (c // 2) % 2
    core = c % 2
    y_lo = h // 4
    z = h % 4

    def at_x(step):
        return (((x + step) % 4) * 4 + y_hi * 2 + core, h)

    def at_z(step):
        return (c, y_lo * 4 + (z + step) % 4)

    x_next, x_prev, x_far = at_x(1), at_x(3), at_x(2)
    y_pair = (x * 4 + (1 - y_hi) * 2 + core, h)
    sibling = (x * 4 + y_hi * 2 + 1 - core, h)
    z_next, z_prev = at_z(1), at_z(3)
    y_mate = (c, (1 - y_lo) * 4 + z)

    barrier = pltpu.get_barrier_semaphore()
    for peer in (x_next, x_prev, x_far, y_pair, sibling, z_next, z_prev, y_mate):
        pl.semaphore_signal(barrier, inc=1, device_id=peer, device_id_type=MESH)

    w_copy = pltpu.make_async_copy(w_hbm, w, w_sem)
    w_copy.start()

    kv[0, 0:TOK, :] = k_ref[...]
    sub16 = lax.broadcasted_iota(jnp.int32, (16, 128), 0)
    for r in range(4):
        base = TOK + r * VROWS
        kv[0, base : base + 128, :] = (
            v_ref[r * 128 : (r + 1) * 128, :].astype(f32).T.astype(bf16)
        )
        id_row = jnp.broadcast_to(ids_ref[r : r + 1, :].astype(f32), (16, 128))
        kv[0, base + 128 : base + VROWS, :] = jnp.where(
            sub16 == 0, 1.0, jnp.where(sub16 == 1, id_row, 0.0)
        ).astype(bf16)

    pl.semaphore_wait(barrier, 8)

    def kv_copy(src, dst, send, peer):
        return pltpu.make_async_remote_copy(
            src_ref=kv.at[src],
            dst_ref=kv.at[dst],
            send_sem=kv_send.at[send],
            recv_sem=kv_recv.at[dst],
            device_id=peer,
            device_id_type=MESH,
        )

    def arrived(slot):
        kv_copy(slot, slot, 0, sibling).wait_recv()

    kv_copy(0, 4, 0, x_next).start()

    @pl.when(y_hi == 0)
    def _():
        kv_copy(0, 2, 2, y_pair).start()

    @pl.when(core == 0)
    def _():
        kv_copy(0, 1, 4, sibling).start()

    lane = lax.broadcasted_iota(jnp.int32, (128, 128), 1).astype(f32)

    def id_columns(slot, r):
        base = TOK + r * VROWS + 128
        row = kv[slot, base : base + 16, :].astype(f32)[1:2, :]
        return jnp.broadcast_to(row, (128, 128)).T

    def key_marks(slot):
        shift = jnp.where(c >= slot, 0.0, 1000.0)
        for r in range(4):
            kf[slot, r * 128 : (r + 1) * 128, :] = jnp.where(
                id_columns(slot, r) + shift == lane, 0.0, FAR
            ).astype(bf16)

    order = (2, 1, 3, 0)
    firsts = [((z + step) % 4) * 64 for step in order]

    for r in range(4):
        kf[0, r * 128 : (r + 1) * 128, :] = jnp.where(id_columns(0, r) == lane, 1.0, 0.0).astype(bf16)
    for t in range(4):
        lo = pl.ds(pl.multiple_of(firsts[t], 64), 64)
        hi = pl.ds(pl.multiple_of(firsts[t] + 256, 64), 64)
        for half, rows in enumerate((lo, hi)):
            marks = kf[0, rows, :]
            for g in range(4):
                for j in range(2):
                    place = j * 128 + half * 64
                    head = 2 * g + j
                    qx[t * 4 + g, place : place + 64, 0:128] = q_ref[rows, head * 128 : (head + 1) * 128]
                    qx[t * 4 + g, place : place + 64, 128:256] = marks
    key_marks(0)

    key_index = lax.broadcasted_iota(jnp.int32, (TOK, 256), 0)
    lane_q = lax.broadcasted_iota(jnp.int32, (1, 256), 1) % 128

    def score(unit, slot, s_ref, mx_ref, diagonal):
        keys = jnp.concatenate([kv[slot, 0:TOK, :], kf[slot]], axis=1)
        s = lax.dot_general(keys, qx[unit], NT, preferred_element_type=f32)
        if diagonal:
            t = unit // 4
            step = jnp.where(t == 0, 2, jnp.where(t == 1, 1, jnp.where(t == 2, 3, 0)))
            first = ((z + step) % 4) * 64
            q_index = first + jnp.where(lane_q < 64, lane_q, lane_q + 192)
            s = jnp.where(key_index <= q_index, s, FAR)
        s_ref[...] = s
        mx_ref[...] = jnp.max(s, axis=0, keepdims=True)

    def gather_values(unit, slot, s_ref, mx_ref, diagonal):
        values = jnp.concatenate(
            [kv[slot, TOK + r * VROWS : TOK + (r + 1) * VROWS, :] for r in range(4)], axis=1
        )
        if diagonal:
            new_top = mx_ref[...]
        else:
            old_top = top[unit]
            new_top = jnp.maximum(old_top, mx_ref[...])
        probs = jnp.exp2((s_ref[...] - new_top) * EXP_SCALE).astype(bf16)
        add = jnp.dot(values, probs, preferred_element_type=f32)
        if diagonal:
            acc[unit] = add
        else:
            acc[unit] = acc[unit] * jnp.exp2((old_top - new_top) * EXP_SCALE) + add
        top[unit] = new_top

    def run(count, unit_of, slot_of, diagonal=False):
        score(unit_of(0), slot_of(0), s0, mx0, diagonal)

        def body(i, carry):
            a, b, n = 2 * i, 2 * i + 1, jnp.minimum(2 * i + 2, count - 1)
            score(unit_of(b), slot_of(b), s1, mx1, diagonal)
            gather_values(unit_of(a), slot_of(a), s0, mx0, diagonal)
            score(unit_of(n), slot_of(n), s0, mx0, diagonal)
            gather_values(unit_of(b), slot_of(b), s1, mx1, diagonal)
            return carry

        lax.fori_loop(0, count // 2, body, 0)

    def one_pass(slot, diagonal=False):
        run(UNITS, lambda i: i, lambda i: slot, diagonal)

    one_pass(0, True)

    arrived(4)
    kv_copy(0, 8, 1, x_far).start()

    @pl.when(y_hi == 0)
    def _():
        kv_copy(4, 6, 3, y_pair).start()

    @pl.when(y_hi == 1)
    def _():
        kv_copy(4, 2, 2, y_pair).start()

    @pl.when(core == 0)
    def _():
        kv_copy(4, 5, 6, sibling).start()

    @pl.when(core == 1)
    def _():
        kv_copy(4, 3, 5, sibling).start()

    key_marks(4)
    one_pass(4)

    arrived(2)

    @pl.when(core == 0)
    def _():
        kv_copy(2, 3, 5, sibling).start()

    @pl.when(core == 1)
    def _():
        kv_copy(2, 1, 4, sibling).start()

    key_marks(2)
    one_pass(2)

    arrived(8)

    @pl.when(y_hi == 1)
    def _():
        kv_copy(8, 6, 3, y_pair).start()

    @pl.when(core == 1)
    def _():
        kv_copy(8, 7, 7, sibling).start()

    key_marks(8)
    one_pass(8)

    arrived(6)

    @pl.when(core == 0)
    def _():
        kv_copy(6, 7, 7, sibling).start()

    @pl.when(core == 1)
    def _():
        kv_copy(6, 5, 6, sibling).start()

    key_marks(6)
    one_pass(6)

    for slot in (1, 3, 5, 7):
        arrived(slot)
        key_marks(slot)

    w_copy.wait()

    def rs_copy(kind, n):
        src, dst, peer = (
            (part.at[0, n, pl.ds(0, 64)], r_a.at[n], z_next),
            (part.at[0, n, pl.ds(64, 64)], r_b.at[n], z_prev),
            (part.at[1, n, pl.ds(64, 64)], r_up.at[n, pl.ds(64, 64)], z_next),
            (part.at[1, n, pl.ds(0, 64)], r_up.at[n, pl.ds(0, 64)], z_next),
            (part.at[2, n, pl.ds(0, 64)], r_down.at[n, pl.ds(0, 64)], z_prev),
            (part.at[2, n, pl.ds(64, 64)], r_down.at[n, pl.ds(64, 64)], z_prev),
            (y_out.at[n], y_in.at[n], y_mate),
        )[kind]
        return pltpu.make_async_remote_copy(
            src_ref=src,
            dst_ref=dst,
            send_sem=rs_send.at[kind, n],
            recv_sem=rs_recv.at[kind, n],
            device_id=peer,
            device_id_type=MESH,
        )

    for t in range(4):
        run(16, lambda i: t * 4 + i // 4, lambda i: 2 * (i % 4) + 1)
        for g in range(4):
            state = acc[t * 4 + g]
            rows = state[0:128] / state[128:129]
            for j in range(2):
                head = 2 * g + j
                att[:, head * 128 : (head + 1) * 128] = rows[:, j * 128 : (j + 1) * 128].T.astype(bf16)

        def project(n, carry):
            cols = pl.ds(pl.multiple_of(n * PCOLS, PCOLS), PCOLS)
            piece = jnp.dot(att[...], w[:, cols], preferred_element_type=f32).astype(bf16)
            if t < 3:
                part[t, n] = piece
            else:
                own[n] = piece
            if t == 0:
                rs_copy(0, n).start()
                rs_copy(1, n).start()
            if t == 1:
                rs_copy(2, n).start()
            if t == 2:
                rs_copy(4, n).start()
            return carry

        lax.fori_loop(0, PIECES, project, 0)

    def pass_on(n, carry):
        rs_copy(0, n).wait_recv()
        part[1, n, 0:64] = (part[1, n, 0:64].astype(f32) + r_a[n].astype(f32)).astype(bf16)
        rs_copy(3, n).start()
        rs_copy(1, n).wait_recv()
        part[2, n, 64:128] = (part[2, n, 64:128].astype(f32) + r_b[n].astype(f32)).astype(bf16)
        rs_copy(5, n).start()
        return carry

    lax.fori_loop(0, PIECES, pass_on, 0)

    def total(n, first):
        rows = pl.ds(pl.multiple_of(first, 64), 64)
        return own[n, rows].astype(f32) + r_up[n, rows].astype(f32) + r_down[n, rows].astype(f32)

    def collect(n, carry):
        for kind in (2, 3, 4, 5):
            rs_copy(kind, n).wait_recv()
        y_out[n] = total(n, 64 - y_lo * 64).astype(bf16)
        rs_copy(6, n).start()
        return carry

    lax.fori_loop(0, PIECES, collect, 0)

    for n in range(PIECES):
        rs_copy(6, n).wait_recv()
        out_ref[:, n * PCOLS : (n + 1) * PCOLS] = (total(n, y_lo * 64) + y_in[n].astype(f32)).astype(bf16)

    for send in range(8):
        kv_copy(0, 0, send, sibling).wait_send()

    def sent(n, carry):
        for kind in range(7):
            rs_copy(kind, n).wait_send()
        return carry

    lax.fori_loop(0, PIECES, sent, 0)


def on_device(queries, key_states, value_states, doc_ids, out_weight):
    vmem = pl.BlockSpec(memory_space=pltpu.VMEM)
    return pl.pallas_call(
        kernel,
        name="attend_project",
        out_shape=jax.ShapeDtypeStruct((64, D_OUT), bf16),
        in_specs=[vmem, vmem, vmem, vmem, pl.BlockSpec(memory_space=pl.ANY)],
        out_specs=vmem,
        scratch_shapes=[
            pltpu.VMEM((SLOTS, BLOCK, 128), bf16),
            pltpu.VMEM((SLOTS, TOK, 128), bf16),
            pltpu.VMEM((UNITS, 256, 256), bf16),
            pltpu.VMEM((TOK, 256), f32),
            pltpu.VMEM((TOK, 256), f32),
            pltpu.VMEM((1, 256), f32),
            pltpu.VMEM((1, 256), f32),
            pltpu.VMEM((UNITS, 1, 256), f32),
            pltpu.VMEM((UNITS, VROWS, 256), f32),
            pltpu.VMEM((128, 1024), bf16),
            pltpu.VMEM((1024, D_OUT), bf16),
            pltpu.VMEM((3, PIECES, 128, PCOLS), bf16),
            pltpu.VMEM((PIECES, 128, PCOLS), bf16),
            pltpu.VMEM((PIECES, 64, PCOLS), bf16),
            pltpu.VMEM((PIECES, 64, PCOLS), bf16),
            pltpu.VMEM((PIECES, 128, PCOLS), bf16),
            pltpu.VMEM((PIECES, 128, PCOLS), bf16),
            pltpu.VMEM((PIECES, 64, PCOLS), bf16),
            pltpu.VMEM((PIECES, 64, PCOLS), bf16),
            pltpu.SemaphoreType.DMA((8,)),
            pltpu.SemaphoreType.DMA((SLOTS,)),
            pltpu.SemaphoreType.DMA((7, PIECES)),
            pltpu.SemaphoreType.DMA((7, PIECES)),
            pltpu.SemaphoreType.DMA,
        ],
        compiler_params=pltpu.CompilerParams(
            collective_id=0, has_side_effects=True, vmem_limit_bytes=56 * 2**20
        ),
        cost_estimate=pl.CostEstimate(
            flops=14 * 10**9, bytes_accessed=10 * 2**20, transcendentals=19 * 10**6
        ),
    )(queries, key_states, value_states, doc_ids.reshape(4, 128), out_weight)


def solution(mesh):
    return jax.shard_map(
        on_device,
        mesh=mesh,
        in_specs=(P("ctx", "head"), P("ctx", "head"), P("ctx", "head"), P("ctx"), P("head", None)),
        out_specs=P(("ctx", "head"), None),
        check_vma=False,
    )
```

time: 418 us -> 88.8 us (0.21)
  waiting for transfers between devices: 172 us -> 0 us
  loops' own time: 120 us -> 0 us
  Pallas kernels: 0 us -> 85.2 us
  local copies, waits for them, and re-layouts: 48.4 us -> 1.87 us
  blocking collectives: 25.7 us -> 0 us
  matrix products: 19 us -> 0 us
  other arithmetic: 18.1 us -> 0 us
  between operations: 13.2 us -> 0.01 us
    another operation x33 -> x0, loops' own time: 120 us -> none  [the longest x1 119 us: on_device(): lax.scan(step_block, (fresh_state(), fresh_state()), blocked)]
    reduce_scatter x1 -> x0, waiting for transfers between devices: 95.8 us -> none  [on_device(): lax.psum_scatter(jnp.dot(attended, out_weight, preferred_element_type=jnp...]
    pallas_call x0 -> x1, Pallas kernels: none -> 85.2 us  [on_device(): pl.pallas_call(kernel, name='attend_project', out_shape=jax.ShapeDtypeStr...]
    all_gather x2 -> x0, waiting for transfers between devices: 74.6 us -> none  [the longest x1 49.6 us: on_device(): value_rows = lax.all_gather(value_states, 'ctx', axis=0, tiled=True)]
    slice x49 -> x0, local copies, waits for them, and re-layouts: 29.9 us -> none  [the longest x32 19.2 us: step_block(): query_pos[-1]]
    all_gather x1 -> x0, blocking collectives: 25.7 us -> none  [on_device(): key_ids = lax.all_gather(doc_ids, 'ctx', axis=0, tiled=True)]
    dot_general x9 -> x0, matrix products: 19 us -> none  [the longest x1 9.48 us: on_device(): jnp.dot(attended, out_weight, preferred_element_type=jnp.float32)]
    squeeze x16 -> x0, local copies, waits for them, and re-layouts: 15.8 us -> none  [on_device(): lax.scan(step_block, (fresh_state(), fresh_state()), blocked)]
  transfers between devices with their start and end apart: 3 -> 0, of which waited for: 3 -> 0; matrix products, arithmetic and copies ran while one was open for 1% -> 0% of each run, Pallas kernels for 0% -> 0%
where the time goes in v1:
time: 88.8 us; the launch traced here: 87.1 us
  Pallas kernels  85.2 us (96%)
  local copies, waits for them, and re-layouts  1.87 us (2%)
    pallas_call x1, Pallas kernels, on_device(): pl.pallas_call(kernel, name='attend_project', out_shape=jax.ShapeDtypeStr...  85.2 us
    unnamed x1, local copies, waits for them, and re-layouts  1.87 us

profile of v1, /device:TPU:1, one launch (start us, length us, event | category | flops | bytes accessed | tf_op | source)
XLA Modules:
  0.0 87.1 jit_solution(12432649602697240210)
XLA Ops:
  0.0 85.2 %attend_project.1 = bf16[64,4096]{1,0:T(8,128)(2,1)} custom-call(bf16[512,1024]{1,0:T(8,128)(2,1)} %q_ref.1, bf16[512,128]{1,0:T(8,128)(2,1)} %k_ref.1, bf16[512,128]{1,0:T(8,128)(2,1)} %v_ref.1, s32[4,128]{1,0:T(4,128)} %bitcast.1, bf16[1024,4096]{1,0:T(8,128)(2,1)} %w_hbm.1), custom_call_target="tpu_custom_call" | custom-call | flops 14000000000 | bytes 10485760 | tf_op jit(solution)/shard_map/attend_project/pallas_call | solution.py:331
  85.2 1.9 %copy.7 = bf16[64,4096]{1,0:T(8,128)(2,1)} copy(bf16[64,4096]{1,0:T(8,128)(2,1)} %attend_project.1) | data formatting | bytes 1048576

commit v2 on v1

v2 whole, which is shorter than its diff:
```python
import jax
import jax.numpy as jnp
from jax import lax
from jax.experimental import pallas as pl
from jax.experimental.pallas import tpu as pltpu
from jax.sharding import PartitionSpec as P

DH = 128
TOK = 512
VROWS = 144
BLOCK = TOK + 4 * VROWS
SLOTS = 9
UNITS = 16
D_OUT = 4096
PCOLS = 512
NY, NZ = 3, 5
EXP_SCALE = DH**-0.5 * 1.4426950408889634
FAR = -1e30
MESH = pl.DeviceIdType.MESH
NT = (((1,), (1,)), ((), ()))
bf16 = jnp.bfloat16
f32 = jnp.float32


def kernel(
    q_ref, k_ref, v_ref, ids_ref, w_hbm, out_ref,
    kv, kf, qx, s0, s1, mx0, mx1, top, acc, att, w,
    part_z, a_z, b_z, up_z, down_z, mate_out, mate_in,
    part_y, met_y, sum_y, a_y, b_y, up_y, down_y,
    kv_send, kv_recv, z_send, z_recv, y_send, y_recv, w_sem,
):
    c = lax.axis_index("ctx")
    h = lax.axis_index("head")
    x = c // 4
    y_hi = (c // 2) % 2
    core = c % 2
    y_lo = h // 4
    z = h % 4

    def at_x(step):
        return (((x + step) % 4) * 4 + y_hi * 2 + core, h)

    def at_z(step):
        return (c, y_lo * 4 + (z + step) % 4)

    x_next, x_prev, x_far = at_x(1), at_x(3), at_x(2)
    y_pair = (x * 4 + (1 - y_hi) * 2 + core, h)
    sibling = (x * 4 + y_hi * 2 + 1 - core, h)
    z_next, z_prev = at_z(1), at_z(3)
    y_mate = (c, (1 - y_lo) * 4 + z)

    barrier = pltpu.get_barrier_semaphore()
    for peer in (x_next, x_prev, x_far, y_pair, sibling, z_next, z_prev, y_mate):
        pl.semaphore_signal(barrier, inc=1, device_id=peer, device_id_type=MESH)

    w_copy = pltpu.make_async_copy(w_hbm, w, w_sem)
    w_copy.start()

    kv[0, 0:TOK, :] = k_ref[...]
    sub16 = lax.broadcasted_iota(jnp.int32, (16, 128), 0)
    for r in range(4):
        base = TOK + r * VROWS
        kv[0, base : base + 128, :] = (
            v_ref[r * 128 : (r + 1) * 128, :].astype(f32).T.astype(bf16)
        )
        id_row = jnp.broadcast_to(ids_ref[r : r + 1, :].astype(f32), (16, 128))
        kv[0, base + 128 : base + VROWS, :] = jnp.where(
            sub16 == 0, 1.0, jnp.where(sub16 == 1, id_row, 0.0)
        ).astype(bf16)

    pl.semaphore_wait(barrier, 8)

    def kv_copy(src, dst, send, peer):
        return pltpu.make_async_remote_copy(
            src_ref=kv.at[src],
            dst_ref=kv.at[dst],
            send_sem=kv_send.at[send],
            recv_sem=kv_recv.at[dst],
            device_id=peer,
            device_id_type=MESH,
        )

    def arrived(slot):
        kv_copy(slot, slot, 0, sibling).wait_recv()

    kv_copy(0, 4, 0, x_next).start()

    @pl.when(y_hi == 0)
    def _():
        kv_copy(0, 2, 2, y_pair).start()

    @pl.when(core == 0)
    def _():
        kv_copy(0, 1, 4, sibling).start()

    lane = lax.broadcasted_iota(jnp.int32, (128, 128), 1).astype(f32)

    def id_columns(slot, r):
        base = TOK + r * VROWS + 128
        row = kv[slot, base : base + 16, :].astype(f32)[1:2, :]
        return jnp.broadcast_to(row, (128, 128)).T

    def key_marks(slot):
        shift = jnp.where(c >= slot, 0.0, 1000.0)
        for r in range(4):
            kf[slot, r * 128 : (r + 1) * 128, :] = jnp.where(
                id_columns(slot, r) + shift == lane, 0.0, FAR
            ).astype(bf16)

    order = (2, 1, 3, 0)
    firsts = [((z + step) % 4) * 64 for step in order]

    for r in range(4):
        kf[0, r * 128 : (r + 1) * 128, :] = jnp.where(id_columns(0, r) == lane, 1.0, 0.0).astype(bf16)
    for t in range(4):
        lo = pl.ds(pl.multiple_of(firsts[t], 64), 64)
        hi = pl.ds(pl.multiple_of(firsts[t] + 256, 64), 64)
        for half, rows in enumerate((lo, hi)):
            marks = kf[0, rows, :]
            for g in range(4):
                for j in range(2):
                    place = j * 128 + half * 64
                    head = 2 * g + j
                    qx[t * 4 + g, place : place + 64, 0:128] = q_ref[rows, head * 128 : (head + 1) * 128]
                    qx[t * 4 + g, place : place + 64, 128:256] = marks
    key_marks(0)

    key_index = lax.broadcasted_iota(jnp.int32, (TOK, 256), 0)
    lane_q = lax.broadcasted_iota(jnp.int32, (1, 256), 1) % 128

    def score(unit, slot, i, s_ref, diagonal):
        keys = jnp.concatenate([kv[slot, 0:TOK, :], kf[slot]], axis=1)
        s = lax.dot_general(keys, qx[unit], NT, preferred_element_type=f32)
        if diagonal:
            t = unit // 4
            step = jnp.where(t == 0, 2, jnp.where(t == 1, 1, jnp.where(t == 2, 3, 0)))
            first = ((z + step) % 4) * 64
            q_index = first + jnp.where(lane_q < 64, lane_q, lane_q + 192)
            s = jnp.where(key_index <= q_index, s, FAR)
        s_ref[i * TOK : (i + 1) * TOK, :] = s
        return jnp.max(s.reshape(TOK // 8, 8, 256), axis=0)

    def weigh(slot, i, s_ref, new_top):
        values = jnp.concatenate(
            [kv[slot, TOK + r * VROWS : TOK + (r + 1) * VROWS, :] for r in range(4)], axis=1
        )
        probs = jnp.exp2((s_ref[i * TOK : (i + 1) * TOK, :] - new_top) * EXP_SCALE).astype(bf16)
        return jnp.dot(values, probs, preferred_element_type=f32)

    def stage(ahead, now, slots, into, held, diagonal):
        if now is not None:
            new_top = jnp.max(held[1][...], axis=0, keepdims=True)
            if not diagonal:
                old_top = top[now]
                new_top = jnp.maximum(old_top, new_top)
        highest, add = None, None
        for i, slot in enumerate(slots):
            if ahead is not None:
                here = score(ahead, slot, i, into[0], diagonal)
                highest = here if highest is None else jnp.maximum(highest, here)
            if now is not None:
                here = weigh(slot, i, held[0], new_top)
                add = here if add is None else add + here
        if ahead is not None:
            into[1][...] = highest
        if now is not None:
            if diagonal:
                acc[now] = add
            else:
                acc[now] = acc[now] * jnp.exp2((old_top - new_top) * EXP_SCALE) + add
            top[now] = new_top

    pair = ((s0, mx0), (s1, mx1))

    def run(first, count, slots, diagonal=False):
        stage(first, None, slots, pair[0], None, diagonal)

        def body(i, carry):
            for e in range(4):
                now = first + 4 * i + e
                ahead = now + 1
                if e == 3:
                    ahead = None if count == 4 else jnp.minimum(ahead, first + count - 1)
                stage(ahead, now, slots, pair[(e + 1) % 2], pair[e % 2], diagonal)
            return carry

        if count == 4:
            body(0, 0)
        else:
            lax.fori_loop(0, count // 4, body, 0)

    run(0, UNITS, (0,), True)

    arrived(4)
    kv_copy(0, 8, 1, x_far).start()

    @pl.when(y_hi == 0)
    def _():
        kv_copy(4, 6, 3, y_pair).start()

    @pl.when(y_hi == 1)
    def _():
        kv_copy(4, 2, 2, y_pair).start()

    @pl.when(core == 0)
    def _():
        kv_copy(4, 5, 6, sibling).start()

    @pl.when(core == 1)
    def _():
        kv_copy(4, 3, 5, sibling).start()

    key_marks(4)
    run(0, UNITS, (4,))

    arrived(2)

    @pl.when(core == 0)
    def _():
        kv_copy(2, 3, 5, sibling).start()

    @pl.when(core == 1)
    def _():
        kv_copy(2, 1, 4, sibling).start()

    key_marks(2)

    arrived(8)

    @pl.when(y_hi == 1)
    def _():
        kv_copy(8, 6, 3, y_pair).start()

    @pl.when(core == 1)
    def _():
        kv_copy(8, 7, 7, sibling).start()

    key_marks(8)
    run(0, UNITS, (2, 8))

    for slot in (1, 3):
        arrived(slot)
        key_marks(slot)

    arrived(6)

    @pl.when(core == 0)
    def _():
        kv_copy(6, 7, 7, sibling).start()

    @pl.when(core == 1)
    def _():
        kv_copy(6, 5, 6, sibling).start()

    key_marks(6)

    for slot in (5, 7):
        arrived(slot)
        key_marks(slot)

    w_copy.wait()

    def z_copy(kind, n):
        low, high = pl.ds(0, 64), pl.ds(64, 64)
        src, dst, peer = (
            (part_z.at[0, n, low], a_z.at[n], z_next),
            (part_z.at[0, n, high], b_z.at[n], z_prev),
            (part_z.at[1, n, high], up_z.at[n, high], z_next),
            (part_z.at[1, n, low], up_z.at[n, low], z_next),
            (part_z.at[2, n, low], down_z.at[n, low], z_prev),
            (part_z.at[2, n, high], down_z.at[n, high], z_prev),
            (mate_out.at[n], mate_in.at[n], y_mate),
        )[kind]
        return pltpu.make_async_remote_copy(
            src_ref=src, dst_ref=dst, send_sem=z_send.at[kind, n], recv_sem=z_recv.at[kind, n],
            device_id=peer, device_id_type=MESH,
        )

    mine = pl.ds(pl.multiple_of(y_lo * 64, 64), 64)
    theirs = pl.ds(pl.multiple_of(64 - y_lo * 64, 64), 64)

    def y_copy(kind, n):
        low, high = pl.ds(0, 32), pl.ds(32, 32)
        if kind < 4:
            src, dst, peer = part_y.at[kind, n, theirs], met_y.at[kind, n], y_mate
        else:
            src, dst, peer = (
                (sum_y.at[0, n, low], a_y.at[n], z_next),
                (sum_y.at[0, n, high], b_y.at[n], z_prev),
                (sum_y.at[1, n, high], up_y.at[n, high], z_next),
                (sum_y.at[1, n, low], up_y.at[n, low], z_next),
                (sum_y.at[2, n, low], down_y.at[n, low], z_prev),
                (sum_y.at[2, n, high], down_y.at[n, high], z_prev),
            )[kind - 4]
        return pltpu.make_async_remote_copy(
            src_ref=src, dst_ref=dst, send_sem=y_send.at[kind, n], recv_sem=y_recv.at[kind, n],
            device_id=peer, device_id_type=MESH,
        )

    def meet(t):
        for n in range(NY):
            y_copy(t, n).wait_recv()
            sum_y[t, n] = (part_y[t, n, mine].astype(f32) + met_y[t, n].astype(f32)).astype(bf16)
            for kind in ((4, 5), (6,), (8,))[t]:
                y_copy(kind, n).start()

    def add_far_z(t):
        for n in range(NZ):
            z_copy(t - 1, n).wait_recv()
            if t == 1:
                part_z[1, n, 0:64] = (part_z[1, n, 0:64].astype(f32) + a_z[n].astype(f32)).astype(bf16)
                z_copy(3, n).start()
            else:
                part_z[2, n, 64:128] = (part_z[2, n, 64:128].astype(f32) + b_z[n].astype(f32)).astype(bf16)
                z_copy(5, n).start()

    def add_far_y(t):
        for n in range(NY):
            y_copy(3 + t, n).wait_recv()
            if t == 1:
                sum_y[1, n, 0:32] = (sum_y[1, n, 0:32].astype(f32) + a_y[n].astype(f32)).astype(bf16)
                y_copy(7, n).start()
            else:
                sum_y[2, n, 32:64] = (sum_y[2, n, 32:64].astype(f32) + b_y[n].astype(f32)).astype(bf16)
                y_copy(9, n).start()

    for t in range(4):
        run(t * 4, 4, (6, 1, 3, 5, 7))
        for g in range(4):
            state = acc[t * 4 + g]
            rows = state[0:128] / state[128:129]
            for j in range(2):
                head = 2 * g + j
                att[:, head * 128 : (head + 1) * 128] = rows[:, j * 128 : (j + 1) * 128].T.astype(bf16)

        for n in range(NY + NZ):
            piece = jnp.dot(
                att[...], w[:, n * PCOLS : (n + 1) * PCOLS], preferred_element_type=f32
            ).astype(bf16)
            if n < NY:
                part_y[t, n] = piece
            else:
                part_z[t, n - NY] = piece
            if n == NY - 1:
                for i in range(NY):
                    y_copy(t, i).start()
        for n in range(NZ):
            for kind in ((0, 1), (2,), (4,), ())[t]:
                z_copy(kind, n).start()
        if t > 0:
            meet(t - 1)
        if t > 1:
            add_far_z(t - 1)

    add_far_y(1)
    add_far_y(2)

    def total_z(n, rows):
        return (
            part_z[3, n, rows].astype(f32) + up_z[n, rows].astype(f32) + down_z[n, rows].astype(f32)
        )

    for n in range(NZ):
        for kind in (2, 3, 4, 5):
            z_copy(kind, n).wait_recv()
        mate_out[n] = total_z(n, theirs).astype(bf16)
        z_copy(6, n).start()

    for n in range(NY):
        for kind in (3, 6, 7, 8, 9):
            y_copy(kind, n).wait_recv()
        out_ref[:, n * PCOLS : (n + 1) * PCOLS] = (
            part_y[3, n, mine].astype(f32) + met_y[3, n].astype(f32)
            + up_y[n].astype(f32) + down_y[n].astype(f32)
        ).astype(bf16)

    for n in range(NZ):
        z_copy(6, n).wait_recv()
        out_ref[:, (NY + n) * PCOLS : (NY + n + 1) * PCOLS] = (
            total_z(n, mine) + mate_in[n].astype(f32)
        ).astype(bf16)

    for send in range(8):
        kv_copy(0, 0, send, sibling).wait_send()
    for n in range(NZ):
        for kind in range(7):
            z_copy(kind, n).wait_send()
    for n in range(NY):
        for kind in range(10):
            y_copy(kind, n).wait_send()


def on_device(queries, key_states, value_states, doc_ids, out_weight):
    vmem = pl.BlockSpec(memory_space=pltpu.VMEM)
    return pl.pallas_call(
        kernel,
        name="attend_project",
        out_shape=jax.ShapeDtypeStruct((64, D_OUT), bf16),
        in_specs=[vmem, vmem, vmem, vmem, pl.BlockSpec(memory_space=pl.ANY)],
        out_specs=vmem,
        scratch_shapes=[
            pltpu.VMEM((SLOTS, BLOCK, 128), bf16),
            pltpu.VMEM((SLOTS, TOK, 128), bf16),
            pltpu.VMEM((UNITS, 256, 256), bf16),
            pltpu.VMEM((5 * TOK, 256), f32),
            pltpu.VMEM((5 * TOK, 256), f32),
            pltpu.VMEM((8, 256), f32),
            pltpu.VMEM((8, 256), f32),
            pltpu.VMEM((UNITS, 1, 256), f32),
            pltpu.VMEM((UNITS, VROWS, 256), f32),
            pltpu.VMEM((128, 1024), bf16),
            pltpu.VMEM((1024, D_OUT), bf16),
            pltpu.VMEM((4, NZ, 128, PCOLS), bf16),
            pltpu.VMEM((NZ, 64, PCOLS), bf16),
            pltpu.VMEM((NZ, 64, PCOLS), bf16),
            pltpu.VMEM((NZ, 128, PCOLS), bf16),
            pltpu.VMEM((NZ, 128, PCOLS), bf16),
            pltpu.VMEM((NZ, 64, PCOLS), bf16),
            pltpu.VMEM((NZ, 64, PCOLS), bf16),
            pltpu.VMEM((4, NY, 128, PCOLS), bf16),
            pltpu.VMEM((4, NY, 64, PCOLS), bf16),
            pltpu.VMEM((3, NY, 64, PCOLS), bf16),
            pltpu.VMEM((NY, 32, PCOLS), bf16),
            pltpu.VMEM((NY, 32, PCOLS), bf16),
            pltpu.VMEM((NY, 64, PCOLS), bf16),
            pltpu.VMEM((NY, 64, PCOLS), bf16),
            pltpu.SemaphoreType.DMA((8,)),
            pltpu.SemaphoreType.DMA((SLOTS,)),
            pltpu.SemaphoreType.DMA((7, NZ)),
            pltpu.SemaphoreType.DMA((7, NZ)),
            pltpu.SemaphoreType.DMA((10, NY)),
            pltpu.SemaphoreType.DMA((10, NY)),
            pltpu.SemaphoreType.DMA,
        ],
        compiler_params=pltpu.CompilerParams(
            collective_id=0, has_side_effects=True, vmem_limit_bytes=56 * 2**20
        ),
        cost_estimate=pl.CostEstimate(
            flops=14 * 10**9, bytes_accessed=10 * 2**20, transcendentals=19 * 10**6
        ),
    )(queries, key_states, value_states, doc_ids.reshape(4, 128), out_weight)


def solution(mesh):
    return jax.shard_map(
        on_device,
        mesh=mesh,
        in_specs=(P("ctx", "head"), P("ctx", "head"), P("ctx", "head"), P("ctx"), P("head", None)),
        out_specs=P(("ctx", "head"), None),
        check_vma=False,
    )
```

time: 88.8 us -> 71.5 us (0.81); the launches traced: 87.1 us -> 71.3 us
  Pallas kernels: 85.2 us -> 69.5 us
    pallas_call x1, Pallas kernels: 85.2 us -> 69.5 us  [on_device(): pl.pallas_call(kernel, name='attend_project', out_shape=jax.ShapeDtypeStr...]
where the time goes in v2:
time: 71.5 us; the launch traced here: 71.3 us
  Pallas kernels  69.5 us (97%)
  local copies, waits for them, and re-layouts  1.87 us (3%)
    pallas_call x1, Pallas kernels, on_device(): pl.pallas_call(kernel, name='attend_project', out_shape=jax.ShapeDtypeStr...  69.5 us
    unnamed x1, local copies, waits for them, and re-layouts  1.87 us

profile of v2, /device:TPU:1, one launch (start us, length us, event | category | flops | bytes accessed | tf_op | source)
XLA Modules:
  0.0 71.3 jit_solution(9547782963514584687)
XLA Ops:
  0.0 69.5 %attend_project.1 = bf16[64,4096]{1,0:T(8,128)(2,1)} custom-call(bf16[512,1024]{1,0:T(8,128)(2,1)} %q_ref.1, bf16[512,128]{1,0:T(8,128)(2,1)} %k_ref.1, bf16[512,128]{1,0:T(8,128)(2,1)} %v_ref.1, s32[4,128]{1,0:T(4,128)} %bitcast.1, bf16[1024,4096]{1,0:T(8,128)(2,1)} %w_hbm.1), custom_call_target="tpu_custom_call" | custom-call | flops 14000000000 | bytes 10485760 | tf_op jit(solution)/shard_map/attend_project/pallas_call | solution.py:395
  69.5 1.9 %copy.7 = bf16[64,4096]{1,0:T(8,128)(2,1)} copy(bf16[64,4096]{1,0:T(8,128)(2,1)} %attend_project.1) | data formatting | bytes 1048576

commit v3 on v2

--- a/solution.py
+++ b/solution.py
@@ -10,6 +10,7 @@
 VROWS = 144
 BLOCK = TOK + 4 * VROWS
 SLOTS = 9
+RELAY_X, RELAY_Y = 9, 10
 UNITS = 16
 D_OUT = 4096
 PCOLS = 512
@@ -23,11 +24,11 @@
 
 
 def kernel(
-    q_ref, k_ref, v_ref, ids_ref, w_hbm, out_ref,
+    q_hbm, k_ref, v_ref, ids_ref, w_hbm, out_ref,
     kv, kf, qx, s0, s1, mx0, mx1, top, acc, att, w,
     part_z, a_z, b_z, up_z, down_z, mate_out, mate_in,
     part_y, met_y, sum_y, a_y, b_y, up_y, down_y,
-    kv_send, kv_recv, z_send, z_recv, y_send, y_recv, w_sem,
+    kv_send, kv_recv, z_send, z_recv, y_send, y_recv, w_sem, q_ref, q_sem,
 ):
     c = lax.axis_index("ctx")
     h = lax.axis_index("head")
@@ -53,6 +54,8 @@
     for peer in (x_next, x_prev, x_far, y_pair, sibling, z_next, z_prev, y_mate):
         pl.semaphore_signal(barrier, inc=1, device_id=peer, device_id_type=MESH)
 
+    q_copy = pltpu.make_async_copy(q_hbm, q_ref, q_sem)
+    q_copy.start()
     w_copy = pltpu.make_async_copy(w_hbm, w, w_sem)
     w_copy.start()
 
@@ -83,15 +86,29 @@
     def arrived(slot):
         kv_copy(slot, slot, 0, sibling).wait_recv()
 
-    kv_copy(0, 4, 0, x_next).start()
-
     @pl.when(y_hi == 0)
     def _():
-        kv_copy(0, 2, 2, y_pair).start()
-
-    @pl.when(core == 0)
-    def _():
-        kv_copy(0, 1, 4, sibling).start()
+        kv_copy(0, 4, 0, x_next).start()
+        kv_copy(0, 2, 1, y_pair).start()
+        kv_copy(0, RELAY_X, 2, x_prev).start()
+
+    @pl.when(y_hi == 1)
+    def _():
+        kv_copy(0, 8, 0, x_far).start()
+        kv_copy(0, RELAY_Y, 1, y_pair).start()
+
+    def share(slot):
+        @pl.when(core == 0)
+        def _():
+            if slot < 8:
+                kv_copy(slot, slot + 1, 6 + slot // 2, sibling).start()
+
+        @pl.when(core == 1)
+        def _():
+            if slot > 0:
+                kv_copy(slot, slot - 1, 5 + slot // 2, sibling).start()
+
+    share(0)
 
     lane = lax.broadcasted_iota(jnp.int32, (128, 128), 1).astype(f32)
 
@@ -109,6 +126,8 @@
 
     order = (2, 1, 3, 0)
     firsts = [((z + step) % 4) * 64 for step in order]
+
+    q_copy.wait()
 
     for r in range(4):
         kf[0, r * 128 : (r + 1) * 128, :] = jnp.where(id_columns(0, r) == lane, 1.0, 0.0).astype(bf16)
@@ -191,71 +210,73 @@
 
     run(0, UNITS, (0,), True)
 
-    arrived(4)
-    kv_copy(0, 8, 1, x_far).start()
-
     @pl.when(y_hi == 0)
     def _():
+        arrived(4)
         kv_copy(4, 6, 3, y_pair).start()
+        share(4)
+        arrived(RELAY_X)
+        kv_copy(RELAY_X, 8, 4, x_prev).start()
+        arrived(RELAY_Y)
+        kv_copy(RELAY_Y, 2, 5, x_next).start()
 
     @pl.when(y_hi == 1)
     def _():
-        kv_copy(4, 2, 2, y_pair).start()
-
-    @pl.when(core == 0)
-    def _():
-        kv_copy(4, 5, 6, sibling).start()
-
-    @pl.when(core == 1)
-    def _():
-        kv_copy(4, 3, 5, sibling).start()
-
-    key_marks(4)
-    run(0, UNITS, (4,))
-
-    arrived(2)
-
-    @pl.when(core == 0)
-    def _():
-        kv_copy(2, 3, 5, sibling).start()
-
-    @pl.when(core == 1)
-    def _():
-        kv_copy(2, 1, 4, sibling).start()
-
-    key_marks(2)
-
-    arrived(8)
+        arrived(8)
+        kv_copy(8, 6, 3, y_pair).start()
+        kv_copy(0, 4, 2, x_next).start()
+        share(8)
+        arrived(2)
+        share(2)
+
+    early = (4 + 4 * y_hi, 2 * y_hi + (1 - y_hi) * (3 + 2 * core))
+    late = (
+        1, 2 + y_hi, 4 * y_hi + (1 - y_hi) * (5 - 2 * core), 6 - y_hi, 7 - y_hi, 8 - y_hi,
+    )
+    key_marks(early[0])
+
+    @pl.when(y_hi == 0)
+    def _():
+        @pl.when(core == 0)
+        def _():
+            arrived(3)
+
+        @pl.when(core == 1)
+        def _():
+            arrived(5)
+
+    key_marks(early[1])
+    run(0, UNITS, early)
+
+    @pl.when(y_hi == 0)
+    def _():
+        arrived(2)
+        share(2)
+        arrived(6)
+        share(6)
+        arrived(8)
+        share(8)
+
+        @pl.when(core == 0)
+        def _():
+            arrived(5)
+
+        @pl.when(core == 1)
+        def _():
+            arrived(3)
 
     @pl.when(y_hi == 1)
     def _():
-        kv_copy(8, 6, 3, y_pair).start()
-
-    @pl.when(core == 1)
-    def _():
-        kv_copy(8, 7, 7, sibling).start()
-
-    key_marks(8)
-    run(0, UNITS, (2, 8))
-
-    for slot in (1, 3):
-        arrived(slot)
-        key_marks(slot)
-
-    arrived(6)
-
-    @pl.when(core == 0)
-    def _():
-        kv_copy(6, 7, 7, sibling).start()
-
-    @pl.when(core == 1)
-    def _():
-        kv_copy(6, 5, 6, sibling).start()
-
-    key_marks(6)
-
-    for slot in (5, 7):
-        arrived(slot)
+        arrived(4)
+        share(4)
+        arrived(6)
+        share(6)
+        arrived(3)
+        arrived(5)
+
+    arrived(1)
+    arrived(7)
+    for slot in late:
         key_marks(slot)
 
     w_copy.wait()
@@ -325,7 +346,7 @@
                 y_copy(9, n).start()
 
     for t in range(4):
-        run(t * 4, 4, (6, 1, 3, 5, 7))
+        run(t * 4, 4, late)
         for g in range(4):
             state = acc[t * 4 + g]
             rows = state[0:128] / state[128:129]
@@ -380,8 +401,14 @@
             total_z(n, mine) + mate_in[n].astype(f32)
         ).astype(bf16)
 
-    for send in range(8):
+    for send in (0, 1, 2, 3, 6, 7, 8, 9):
         kv_copy(0, 0, send, sibling).wait_send()
+
+    @pl.when(y_hi == 0)
+    def _():
+        for send in (4, 5):
+            kv_copy(0, 0, send, sibling).wait_send()
+
     for n in range(NZ):
         for kind in range(7):
             z_copy(kind, n).wait_send()
@@ -396,14 +423,14 @@
         kernel,
         name="attend_project",
         out_shape=jax.ShapeDtypeStruct((64, D_OUT), bf16),
-        in_specs=[vmem, vmem, vmem, vmem, pl.BlockSpec(memory_space=pl.ANY)],
+        in_specs=[pl.BlockSpec(memory_space=pl.ANY), vmem, vmem, vmem, pl.BlockSpec(memory_space=pl.ANY)],
         out_specs=vmem,
         scratch_shapes=[
-            pltpu.VMEM((SLOTS, BLOCK, 128), bf16),
+            pltpu.VMEM((SLOTS + 2, BLOCK, 128), bf16),
             pltpu.VMEM((SLOTS, TOK, 128), bf16),
             pltpu.VMEM((UNITS, 256, 256), bf16),
-            pltpu.VMEM((5 * TOK, 256), f32),
-            pltpu.VMEM((5 * TOK, 256), f32),
+            pltpu.VMEM((6 * TOK, 256), f32),
+            pltpu.VMEM((6 * TOK, 256), f32),
             pltpu.VMEM((8, 256), f32),
             pltpu.VMEM((8, 256), f32),
             pltpu.VMEM((UNITS, 1, 256), f32),
@@ -424,12 +451,14 @@
             pltpu.VMEM((NY, 32, PCOLS), bf16),
             pltpu.VMEM((NY, 64, PCOLS), bf16),
             pltpu.VMEM((NY, 64, PCOLS), bf16),
-            pltpu.SemaphoreType.DMA((8,)),
-            pltpu.SemaphoreType.DMA((SLOTS,)),
+            pltpu.SemaphoreType.DMA((10,)),
+            pltpu.SemaphoreType.DMA((SLOTS + 2,)),
             pltpu.SemaphoreType.DMA((7, NZ)),
             pltpu.SemaphoreType.DMA((7, NZ)),
             pltpu.SemaphoreType.DMA((10, NY)),
             pltpu.SemaphoreType.DMA((10, NY)),
+            pltpu.SemaphoreType.DMA,
+            pltpu.VMEM((TOK, 1024), bf16),
             pltpu.SemaphoreType.DMA,
         ],
         compiler_params=pltpu.CompilerParams(

time: 71.5 us -> 65.9 us (0.922)
  Pallas kernels: 69.5 us -> 63.9 us
    pallas_call x1, Pallas kernels: 69.5 us -> 63.9 us  [on_device(): pl.pallas_call(kernel, name='attend_project', out_shape=jax.ShapeDtypeStr...]
where the time goes in v3:
time: 65.9 us; the launch traced here: 65.7 us
  Pallas kernels  63.9 us (97%)
  local copies, waits for them, and re-layouts  1.87 us (3%)
    pallas_call x1, Pallas kernels, on_device(): pl.pallas_call(kernel, name='attend_project', out_shape=jax.ShapeDtypeStr...  63.9 us
    unnamed x1, local copies, waits for them, and re-layouts  1.87 us

profile of v3, /device:TPU:1, one launch (start us, length us, event | category | flops | bytes accessed | tf_op | source)
XLA Modules:
  0.0 65.7 jit_solution(7445918404935996414)
XLA Ops:
  0.0 63.9 %attend_project.1 = bf16[64,4096]{1,0:T(8,128)(2,1)} custom-call(bf16[512,1024]{1,0:T(8,128)(2,1)} %q_hbm.1, bf16[512,128]{1,0:T(8,128)(2,1)} %k_ref.1, bf16[512,128]{1,0:T(8,128)(2,1)} %v_ref.1, s32[4,128]{1,0:T(4,128)} %bitcast.1, bf16[1024,4096]{1,0:T(8,128)(2,1)} %w_hbm.1), custom_call_target="tpu_custom_call" | custom-call | flops 14000000000 | bytes 10485760 | tf_op jit(solution)/shard_map/attend_project/pallas_call | solution.py:422
  63.9 1.9 %copy.7 = bf16[64,4096]{1,0:T(8,128)(2,1)} copy(bf16[64,4096]{1,0:T(8,128)(2,1)} %attend_project.1) | data formatting | bytes 1048576

commit v4 on v3

--- a/solution.py
+++ b/solution.py
@@ -14,7 +14,7 @@
 UNITS = 16
 D_OUT = 4096
 PCOLS = 512
-NY, NZ = 3, 5
+NY, NZ = 4, 4
 EXP_SCALE = DH**-0.5 * 1.4426950408889634
 FAR = -1e30
 MESH = pl.DeviceIdType.MESH
@@ -27,7 +27,7 @@
     q_hbm, k_ref, v_ref, ids_ref, w_hbm, out_ref,
     kv, kf, qx, s0, s1, mx0, mx1, top, acc, att, w,
     part_z, a_z, b_z, up_z, down_z, mate_out, mate_in,
-    part_y, met_y, sum_y, a_y, b_y, up_y, down_y,
+    part_y, met_y, sum_y, far_y, near_y,
     kv_send, kv_recv, z_send, z_recv, y_send, y_recv, w_sem, q_ref, q_sem,
 ):
     c = lax.axis_index("ctx")
@@ -124,17 +124,16 @@
                 id_columns(slot, r) + shift == lane, 0.0, FAR
             ).astype(bf16)
 
-    order = (2, 1, 3, 0)
-    firsts = [((z + step) % 4) * 64 for step in order]
+    order = ((2, 2), (3, 1), (1, 3), (0, 0))
+    firsts = [(((z + low) % 4) * 64, ((z + high) % 4) * 64 + 256) for low, high in order]
 
     q_copy.wait()
 
     for r in range(4):
         kf[0, r * 128 : (r + 1) * 128, :] = jnp.where(id_columns(0, r) == lane, 1.0, 0.0).astype(bf16)
     for t in range(4):
-        lo = pl.ds(pl.multiple_of(firsts[t], 64), 64)
-        hi = pl.ds(pl.multiple_of(firsts[t] + 256, 64), 64)
-        for half, rows in enumerate((lo, hi)):
+        for half in range(2):
+            rows = pl.ds(pl.multiple_of(firsts[t][half], 64), 64)
             marks = kf[0, rows, :]
             for g in range(4):
                 for j in range(2):
@@ -152,9 +151,11 @@
         s = lax.dot_general(keys, qx[unit], NT, preferred_element_type=f32)
         if diagonal:
             t = unit // 4
-            step = jnp.where(t == 0, 2, jnp.where(t == 1, 1, jnp.where(t == 2, 3, 0)))
-            first = ((z + step) % 4) * 64
-            q_index = first + jnp.where(lane_q < 64, lane_q, lane_q + 192)
+            low = jnp.where(t == 0, 2, jnp.where(t == 1, 3, jnp.where(t == 2, 1, 0)))
+            high = jnp.where(t == 0, 2, jnp.where(t == 1, 1, jnp.where(t == 2, 3, 0)))
+            low_first = ((z + low) % 4) * 64
+            high_first = ((z + high) % 4) * 64 + 192
+            q_index = lane_q + jnp.where(lane_q < 64, low_first, high_first)
             s = jnp.where(key_index <= q_index, s, FAR)
         s_ref[i * TOK : (i + 1) * TOK, :] = s
         return jnp.max(s.reshape(TOK // 8, 8, 256), axis=0)
@@ -231,7 +232,7 @@
 
     early = (4 + 4 * y_hi, 2 * y_hi + (1 - y_hi) * (3 + 2 * core))
     late = (
-        1, 2 + y_hi, 4 * y_hi + (1 - y_hi) * (5 - 2 * core), 6 - y_hi, 7 - y_hi, 8 - y_hi,
+        2 - y_hi, 6 - 2 * y_hi, 8 - 2 * y_hi, 1 + 2 * y_hi, 5 - 2 * core * (1 - y_hi), 7,
     )
     key_marks(early[0])
 
@@ -257,27 +258,38 @@
         arrived(8)
         share(8)
 
-        @pl.when(core == 0)
-        def _():
-            arrived(5)
-
-        @pl.when(core == 1)
-        def _():
-            arrived(3)
-
     @pl.when(y_hi == 1)
     def _():
         arrived(4)
         share(4)
         arrived(6)
         share(6)
-        arrived(3)
-        arrived(5)
-
-    arrived(1)
-    arrived(7)
-    for slot in late:
+        arrived(1)
+
+    for slot in late[:3]:
         key_marks(slot)
+
+    def arrive_last():
+        @pl.when(y_hi == 0)
+        def _():
+            arrived(1)
+
+            @pl.when(core == 0)
+            def _():
+                arrived(5)
+
+            @pl.when(core == 1)
+            def _():
+                arrived(3)
+
+        @pl.when(y_hi == 1)
+        def _():
+            arrived(3)
+            arrived(5)
+
+        arrived(7)
+        for slot in late[3:]:
+            key_marks(slot)
 
     w_copy.wait()
 
@@ -287,8 +299,8 @@
             (part_z.at[0, n, low], a_z.at[n], z_next),
             (part_z.at[0, n, high], b_z.at[n], z_prev),
             (part_z.at[1, n, high], up_z.at[n, high], z_next),
-            (part_z.at[1, n, low], up_z.at[n, low], z_next),
-            (part_z.at[2, n, low], down_z.at[n, low], z_prev),
+            (part_z.at[2, n, low], up_z.at[n, low], z_next),
+            (part_z.at[1, n, low], down_z.at[n, low], z_prev),
             (part_z.at[2, n, high], down_z.at[n, high], z_prev),
             (mate_out.at[n], mate_in.at[n], y_mate),
         )[kind]
@@ -300,21 +312,27 @@
     mine = pl.ds(pl.multiple_of(y_lo * 64, 64), 64)
     theirs = pl.ds(pl.multiple_of(64 - y_lo * 64, 64), 64)
 
+    def way(t):
+        return (t + y_lo) % 2
+
+    def half_of(t, with_far):
+        first = 32 * way(t) if with_far else 32 - 32 * way(t)
+        return pl.ds(pl.multiple_of(first, 32), 32)
+
     def y_copy(kind, n):
-        low, high = pl.ds(0, 32), pl.ds(32, 32)
+        place = kind
         if kind < 4:
             src, dst, peer = part_y.at[kind, n, theirs], met_y.at[kind, n], y_mate
+        elif kind < 6:
+            src = sum_y.at[0, n, pl.ds(32 * (kind - 4), 32)]
+            dst, peer = far_y.at[kind - 4, n], (z_next, z_prev)[kind - 4]
         else:
-            src, dst, peer = (
-                (sum_y.at[0, n, low], a_y.at[n], z_next),
-                (sum_y.at[0, n, high], b_y.at[n], z_prev),
-                (sum_y.at[1, n, high], up_y.at[n, high], z_next),
-                (sum_y.at[1, n, low], up_y.at[n, low], z_next),
-                (sum_y.at[2, n, low], down_y.at[n, low], z_prev),
-                (sum_y.at[2, n, high], down_y.at[n, high], z_prev),
-            )[kind - 4]
+            t, with_far = kind // 2 - 2, kind % 2
+            rows = half_of(t, with_far)
+            src, dst, peer = sum_y.at[t, n, rows], near_y.at[way(t), n, rows], at_z(1 + 2 * way(t))
+            place = 6 + 2 * way(t) + with_far
         return pltpu.make_async_remote_copy(
-            src_ref=src, dst_ref=dst, send_sem=y_send.at[kind, n], recv_sem=y_recv.at[kind, n],
+            src_ref=src, dst_ref=dst, send_sem=y_send.at[kind, n], recv_sem=y_recv.at[place, n],
             device_id=peer, device_id_type=MESH,
         )
 
@@ -325,28 +343,33 @@
             for kind in ((4, 5), (6,), (8,))[t]:
                 y_copy(kind, n).start()
 
-    def add_far_z(t):
+    def add_far_z():
         for n in range(NZ):
-            z_copy(t - 1, n).wait_recv()
-            if t == 1:
-                part_z[1, n, 0:64] = (part_z[1, n, 0:64].astype(f32) + a_z[n].astype(f32)).astype(bf16)
-                z_copy(3, n).start()
-            else:
-                part_z[2, n, 64:128] = (part_z[2, n, 64:128].astype(f32) + b_z[n].astype(f32)).astype(bf16)
-                z_copy(5, n).start()
-
-    def add_far_y(t):
+            z_copy(0, n).wait_recv()
+            part_z[2, n, 0:64] = (part_z[2, n, 0:64].astype(f32) + a_z[n].astype(f32)).astype(bf16)
+            z_copy(3, n).start()
+            z_copy(1, n).wait_recv()
+            part_z[2, n, 64:128] = (part_z[2, n, 64:128].astype(f32) + b_z[n].astype(f32)).astype(bf16)
+            z_copy(5, n).start()
+
+    def add_far_y():
         for n in range(NY):
-            y_copy(3 + t, n).wait_recv()
-            if t == 1:
-                sum_y[1, n, 0:32] = (sum_y[1, n, 0:32].astype(f32) + a_y[n].astype(f32)).astype(bf16)
-                y_copy(7, n).start()
-            else:
-                sum_y[2, n, 32:64] = (sum_y[2, n, 32:64].astype(f32) + b_y[n].astype(f32)).astype(bf16)
-                y_copy(9, n).start()
+            y_copy(4, n).wait_recv()
+            y_copy(5, n).wait_recv()
+            for t in (1, 2):
+                rows = half_of(t, 1)
+                sum_y[t, n, rows] = (
+                    sum_y[t, n, rows].astype(f32) + far_y[way(t), n].astype(f32)
+                ).astype(bf16)
+                y_copy(5 + 2 * t, n).start()
 
     for t in range(4):
-        run(t * 4, 4, late)
+        if t == 0:
+            run(0, 4, late[:3])
+            arrive_last()
+            run(0, 4, late[3:])
+        else:
+            run(t * 4, 4, late)
         for g in range(4):
             state = acc[t * 4 + g]
             rows = state[0:128] / state[128:129]
@@ -366,15 +389,14 @@
                 for i in range(NY):
                     y_copy(t, i).start()
         for n in range(NZ):
-            for kind in ((0, 1), (2,), (4,), ())[t]:
+            for kind in ((0, 1), (2, 4), (), ())[t]:
                 z_copy(kind, n).start()
         if t > 0:
             meet(t - 1)
-        if t > 1:
-            add_far_z(t - 1)
-
-    add_far_y(1)
-    add_far_y(2)
+        if t == 2:
+            add_far_z()
+
+    add_far_y()
 
     def total_z(n, rows):
         return (
@@ -392,7 +414,7 @@
             y_copy(kind, n).wait_recv()
         out_ref[:, n * PCOLS : (n + 1) * PCOLS] = (
             part_y[3, n, mine].astype(f32) + met_y[3, n].astype(f32)
-            + up_y[n].astype(f32) + down_y[n].astype(f32)
+            + near_y[0, n].astype(f32) + near_y[1, n].astype(f32)
         ).astype(bf16)
 
     for n in range(NZ):
@@ -447,10 +469,8 @@
             pltpu.VMEM((4, NY, 128, PCOLS), bf16),
             pltpu.VMEM((4, NY, 64, PCOLS), bf16),
             pltpu.VMEM((3, NY, 64, PCOLS), bf16),
-            pltpu.VMEM((NY, 32, PCOLS), bf16),
-            pltpu.VMEM((NY, 32, PCOLS), bf16),
-            pltpu.VMEM((NY, 64, PCOLS), bf16),
-            pltpu.VMEM((NY, 64, PCOLS), bf16),
+            pltpu.VMEM((2, NY, 32, PCOLS), bf16),
+            pltpu.VMEM((2, NY, 64, PCOLS), bf16),
             pltpu.SemaphoreType.DMA((10,)),
             pltpu.SemaphoreType.DMA((SLOTS + 2,)),
             pltpu.SemaphoreType.DMA((7, NZ)),

time: 65.9 us -> 62.5 us (0.948); the launches traced: 65.7 us -> 61.5 us
  Pallas kernels: 63.9 us -> 59.6 us
    pallas_call x1, Pallas kernels: 63.9 us -> 59.6 us  [on_device(): pl.pallas_call(kernel, name='attend_project', out_shape=jax.ShapeDtypeStr...]
where the time goes in v4:
time: 62.5 us; the launch traced here: 61.5 us
  Pallas kernels  59.6 us (95%)
  local copies, waits for them, and re-layouts  1.87 us (3%)
    pallas_call x1, Pallas kernels, on_device(): pl.pallas_call(kernel, name='attend_project', out_shape=jax.ShapeDtypeStr...  59.6 us
    unnamed x1, local copies, waits for them, and re-layouts  1.87 us

profile of v4, /device:TPU:1, one launch (start us, length us, event | category | flops | bytes accessed | tf_op | source)
XLA Modules:
  0.0 61.5 jit_solution(11974598526441650230)
XLA Ops:
  0.0 59.6 %attend_project.1 = bf16[64,4096]{1,0:T(8,128)(2,1)} custom-call(bf16[512,1024]{1,0:T(8,128)(2,1)} %q_hbm.1, bf16[512,128]{1,0:T(8,128)(2,1)} %k_ref.1, bf16[512,128]{1,0:T(8,128)(2,1)} %v_ref.1, s32[4,128]{1,0:T(4,128)} %bitcast.1, bf16[1024,4096]{1,0:T(8,128)(2,1)} %w_hbm.1), custom_call_target="tpu_custom_call" | custom-call | flops 14000000000 | bytes 10485760 | tf_op jit(solution)/shard_map/attend_project/pallas_call | solution.py:444
  59.6 1.9 %copy.7 = bf16[64,4096]{1,0:T(8,128)(2,1)} copy(bf16[64,4096]{1,0:T(8,128)(2,1)} %attend_project.1) | data formatting | bytes 1048576

commit v5 on v4

--- a/solution.py
+++ b/solution.py
@@ -8,7 +8,8 @@
 DH = 128
 TOK = 512
 VROWS = 144
-BLOCK = TOK + 4 * VROWS
+IDS = 2 * TOK
+BLOCK = IDS + 16
 SLOTS = 9
 RELAY_X, RELAY_Y = 9, 10
 UNITS = 16
@@ -24,11 +25,11 @@
 
 
 def kernel(
-    q_hbm, k_ref, v_ref, ids_ref, w_hbm, out_ref,
+    q_hbm, k_hbm, v_hbm, ids_hbm, w_hbm, one_ref, two_ref,
     kv, kf, qx, s0, s1, mx0, mx1, top, acc, att, w,
     part_z, a_z, b_z, up_z, down_z, mate_out, mate_in,
     part_y, met_y, sum_y, far_y, near_y,
-    kv_send, kv_recv, z_send, z_recv, y_send, y_recv, w_sem, q_ref, q_sem,
+    kv_send, kv_recv, z_send, z_recv, y_send, y_recv, w_sem, q_ref, v_ref, ids_ref, in_sem,
 ):
     c = lax.axis_index("ctx")
     h = lax.axis_index("head")
@@ -50,26 +51,31 @@
     z_next, z_prev = at_z(1), at_z(3)
     y_mate = (c, (1 - y_lo) * 4 + z)
 
+    ids_copy = pltpu.make_async_copy(ids_hbm, ids_ref, in_sem.at[0])
+    ids_copy.start()
+    v_copy = pltpu.make_async_copy(v_hbm, v_ref, in_sem.at[1])
+    v_copy.start()
+    k_copy = pltpu.make_async_copy(k_hbm, kv.at[0, pl.ds(0, TOK)], in_sem.at[2])
+    k_copy.start()
+    q_copy = pltpu.make_async_copy(q_hbm, q_ref, in_sem.at[3])
+    q_copy.start()
+    w_copy = pltpu.make_async_copy(w_hbm, w, w_sem)
+    w_copy.start()
+
     barrier = pltpu.get_barrier_semaphore()
     for peer in (x_next, x_prev, x_far, y_pair, sibling, z_next, z_prev, y_mate):
         pl.semaphore_signal(barrier, inc=1, device_id=peer, device_id_type=MESH)
 
-    q_copy = pltpu.make_async_copy(q_hbm, q_ref, q_sem)
-    q_copy.start()
-    w_copy = pltpu.make_async_copy(w_hbm, w, w_sem)
-    w_copy.start()
-
-    kv[0, 0:TOK, :] = k_ref[...]
-    sub16 = lax.broadcasted_iota(jnp.int32, (16, 128), 0)
+    ids_copy.wait()
+    kv[0, IDS:BLOCK, :] = jnp.concatenate(
+        [ids_ref[...].astype(f32), jnp.zeros((12, 128), f32)], axis=0
+    ).astype(bf16)
+    v_copy.wait()
     for r in range(4):
-        base = TOK + r * VROWS
-        kv[0, base : base + 128, :] = (
+        kv[0, TOK + r * 128 : TOK + (r + 1) * 128, :] = (
             v_ref[r * 128 : (r + 1) * 128, :].astype(f32).T.astype(bf16)
         )
-        id_row = jnp.broadcast_to(ids_ref[r : r + 1, :].astype(f32), (16, 128))
-        kv[0, base + 128 : base + VROWS, :] = jnp.where(
-            sub16 == 0, 1.0, jnp.where(sub16 == 1, id_row, 0.0)
-        ).astype(bf16)
+    k_copy.wait()
 
     pl.semaphore_wait(barrier, 8)
 
@@ -113,8 +119,7 @@
     lane = lax.broadcasted_iota(jnp.int32, (128, 128), 1).astype(f32)
 
     def id_columns(slot, r):
-        base = TOK + r * VROWS + 128
-        row = kv[slot, base : base + 16, :].astype(f32)[1:2, :]
+        row = kv[slot, IDS:BLOCK, :].astype(f32)[r : r + 1, :]
         return jnp.broadcast_to(row, (128, 128)).T
 
     def key_marks(slot):
@@ -143,6 +148,7 @@
                     qx[t * 4 + g, place : place + 64, 128:256] = marks
     key_marks(0)
 
+    ones = jnp.ones((VROWS - 128, TOK), bf16)
     key_index = lax.broadcasted_iota(jnp.int32, (TOK, 256), 0)
     lane_q = lax.broadcasted_iota(jnp.int32, (1, 256), 1) % 128
 
@@ -162,8 +168,9 @@
 
     def weigh(slot, i, s_ref, new_top):
         values = jnp.concatenate(
-            [kv[slot, TOK + r * VROWS : TOK + (r + 1) * VROWS, :] for r in range(4)], axis=1
+            [kv[slot, TOK + r * 128 : TOK + (r + 1) * 128, :] for r in range(4)], axis=1
         )
+        values = jnp.concatenate([values, ones], axis=0)
         probs = jnp.exp2((s_ref[i * TOK : (i + 1) * TOK, :] - new_top) * EXP_SCALE).astype(bf16)
         return jnp.dot(values, probs, preferred_element_type=f32)
 
@@ -388,9 +395,10 @@
             if n == NY - 1:
                 for i in range(NY):
                     y_copy(t, i).start()
-        for n in range(NZ):
-            for kind in ((0, 1), (2, 4), (), ())[t]:
-                z_copy(kind, n).start()
+            if n == NY + 1 or n == NY + 3:
+                for i in (n - NY - 1, n - NY):
+                    for kind in ((0, 1), (2, 4), (), ())[t]:
+                        z_copy(kind, i).start()
         if t > 0:
             meet(t - 1)
         if t == 2:
@@ -409,19 +417,25 @@
         mate_out[n] = total_z(n, theirs).astype(bf16)
         z_copy(6, n).start()
 
+    for n in range(NZ):
+        one_ref[:, (NY + n) * PCOLS : (NY + n + 1) * PCOLS] = total_z(n, mine).astype(bf16)
+
     for n in range(NY):
-        for kind in (3, 6, 7, 8, 9):
+        y_copy(3, n).wait_recv()
+        one_ref[:, n * PCOLS : (n + 1) * PCOLS] = (
+            part_y[3, n, mine].astype(f32) + met_y[3, n].astype(f32)
+        ).astype(bf16)
+
+    for n in range(NY):
+        for kind in (6, 7, 8, 9):
             y_copy(kind, n).wait_recv()
-        out_ref[:, n * PCOLS : (n + 1) * PCOLS] = (
-            part_y[3, n, mine].astype(f32) + met_y[3, n].astype(f32)
-            + near_y[0, n].astype(f32) + near_y[1, n].astype(f32)
+        two_ref[:, n * PCOLS : (n + 1) * PCOLS] = (
+            near_y[0, n].astype(f32) + near_y[1, n].astype(f32)
         ).astype(bf16)
 
     for n in range(NZ):
         z_copy(6, n).wait_recv()
-        out_ref[:, (NY + n) * PCOLS : (NY + n + 1) * PCOLS] = (
-            total_z(n, mine) + mate_in[n].astype(f32)
-        ).astype(bf16)
+        two_ref[:, (NY + n) * PCOLS : (NY + n + 1) * PCOLS] = mate_in[n]
 
     for send in (0, 1, 2, 3, 6, 7, 8, 9):
         kv_copy(0, 0, send, sibling).wait_send()
@@ -441,12 +455,12 @@
 
 def on_device(queries, key_states, value_states, doc_ids, out_weight):
     vmem = pl.BlockSpec(memory_space=pltpu.VMEM)
-    return pl.pallas_call(
+    one, two = pl.pallas_call(
         kernel,
         name="attend_project",
-        out_shape=jax.ShapeDtypeStruct((64, D_OUT), bf16),
-        in_specs=[pl.BlockSpec(memory_space=pl.ANY), vmem, vmem, vmem, pl.BlockSpec(memory_space=pl.ANY)],
-        out_specs=vmem,
+        out_shape=[jax.ShapeDtypeStruct((64, D_OUT), bf16)] * 2,
+        in_specs=[pl.BlockSpec(memory_space=pl.ANY)] * 5,
+        out_specs=[vmem, vmem],
         scratch_shapes=[
             pltpu.VMEM((SLOTS + 2, BLOCK, 128), bf16),
             pltpu.VMEM((SLOTS, TOK, 128), bf16),
@@ -479,7 +493,9 @@
             pltpu.SemaphoreType.DMA((10, NY)),
             pltpu.SemaphoreType.DMA,
             pltpu.VMEM((TOK, 1024), bf16),
-            pltpu.SemaphoreType.DMA,
+            pltpu.VMEM((TOK, 128), bf16),
+            pltpu.VMEM((4, 128), jnp.int32),
+            pltpu.SemaphoreType.DMA((4,)),
         ],
         compiler_params=pltpu.CompilerParams(
             collective_id=0, has_side_effects=True, vmem_limit_bytes=56 * 2**20
@@ -488,6 +504,7 @@
             flops=14 * 10**9, bytes_accessed=10 * 2**20, transcendentals=19 * 10**6
         ),
     )(queries, key_states, value_states, doc_ids.reshape(4, 128), out_weight)
+    return (one.astype(f32) + two.astype(f32)).astype(bf16)
 
 
 def solution(mesh):

time: 62.5 us -> 61.3 us (0.981); the launches traced: 61.5 us -> 61.1 us
  other arithmetic: 0 us -> 2.12 us
  local copies, waits for them, and re-layouts: 1.87 us -> 0 us
    convert_element_type x0 -> x1, other arithmetic: none -> 2.12 us  [on_device(): return (one.astype(f32) + two.astype(f32)).astype(bf16)]
    unnamed x1 -> x0, local copies, waits for them, and re-layouts: 1.87 us -> none
where the time goes in v5:
time: 61.3 us; the launch traced here: 61.1 us
  Pallas kernels  59 us (96%)
  other arithmetic  2.12 us (3%)
    pallas_call x1, Pallas kernels, on_device(): pl.pallas_call(kernel, name='attend_project', out_shape=[jax.ShapeDtypeSt...  59 us
    convert_element_type x1, other arithmetic, on_device(): return (one.astype(f32) + two.astype(f32)).astype(bf16)  2.12 us

profile of v5, /device:TPU:1, one launch (start us, length us, event | category | flops | bytes accessed | tf_op | source)
XLA Modules:
  0.0 61.1 jit_solution(13232945140753840343)
XLA Ops:
  0.0 59.0 %attend_project.1 = (bf16[64,4096]{1,0:T(8,128)(2,1)}, bf16[64,4096]{1,0:T(8,128)(2,1)}) custom-call(bf16[512,1024]{1,0:T(8,128)(2,1)} %q_hbm.1, bf16[512,128]{1,0:T(8,128)(2,1)} %k_hbm.1, bf16[512,128]{1,0:T(8,128)(2,1)} %v_hbm.1, s32[4,128]{1,0:T(4,128)} %bitcast.1, bf16[1024,4096]{1,0:T(8,128)(2,1)} %w_hbm.1), custom_call_target="tpu_custom_call" | custom-call | flops 14000000000 | bytes 10485760 | tf_op jit(solution)/shard_map/attend_project/pallas_call | solution.py:458
  59.0 2.1 %add_convert_fusion = bf16[64,4096]{1,0:T(8,128)(2,1)} fusion(bf16[64,4096]{1,0:T(8,128)(2,1)} %get-tuple-element.8, bf16[64,4096]{1,0:T(8,128)(2,1)} %get-tuple-element.7), kind=kLoop, calls=%fused_computation | loop fusion | flops 1048576 | bytes 1572864 | tf_op jit(solution)/shard_map/convert_element_type | solution.py:507

commit v6 on v5

--- a/solution.py
+++ b/solution.py
@@ -79,42 +79,47 @@
 
     pl.semaphore_wait(barrier, 8)
 
-    def kv_copy(src, dst, send, peer):
+    def kv_copy(src, dst, send, peer, half):
+        rows = (pl.ds(0, TOK), pl.ds(TOK, BLOCK - TOK))[half]
         return pltpu.make_async_remote_copy(
-            src_ref=kv.at[src],
-            dst_ref=kv.at[dst],
-            send_sem=kv_send.at[send],
-            recv_sem=kv_recv.at[dst],
+            src_ref=kv.at[src, rows],
+            dst_ref=kv.at[dst, rows],
+            send_sem=kv_send.at[send, half],
+            recv_sem=kv_recv.at[dst, half],
             device_id=peer,
             device_id_type=MESH,
         )
 
-    def arrived(slot):
-        kv_copy(slot, slot, 0, sibling).wait_recv()
+    def arrived(slot, half=None):
+        for part_of in (0, 1) if half is None else (half,):
+            kv_copy(slot, slot, 0, sibling, part_of).wait_recv()
 
     @pl.when(y_hi == 0)
     def _():
-        kv_copy(0, 4, 0, x_next).start()
-        kv_copy(0, 2, 1, y_pair).start()
-        kv_copy(0, RELAY_X, 2, x_prev).start()
+        for half in range(2):
+            kv_copy(0, 4, 0, x_next, half).start()
+            kv_copy(0, 2, 1, y_pair, half).start()
+            kv_copy(0, RELAY_X, 2, x_prev, half).start()
 
     @pl.when(y_hi == 1)
     def _():
-        kv_copy(0, 8, 0, x_far).start()
-        kv_copy(0, RELAY_Y, 1, y_pair).start()
-
-    def share(slot):
+        for half in range(2):
+            kv_copy(0, 8, 0, x_far, half).start()
+            kv_copy(0, RELAY_Y, 1, y_pair, half).start()
+
+    def share(slot, half):
         @pl.when(core == 0)
         def _():
             if slot < 8:
-                kv_copy(slot, slot + 1, 6 + slot // 2, sibling).start()
+                kv_copy(slot, slot + 1, 6 + slot // 2, sibling, half).start()
 
         @pl.when(core == 1)
         def _():
             if slot > 0:
-                kv_copy(slot, slot - 1, 5 + slot // 2, sibling).start()
-
-    share(0)
+                kv_copy(slot, slot - 1, 5 + slot // 2, sibling, half).start()
+
+    share(0, 0)
+    share(0, 1)
 
     lane = lax.broadcasted_iota(jnp.int32, (128, 128), 1).astype(f32)
 
@@ -220,22 +225,24 @@
 
     @pl.when(y_hi == 0)
     def _():
-        arrived(4)
-        kv_copy(4, 6, 3, y_pair).start()
-        share(4)
-        arrived(RELAY_X)
-        kv_copy(RELAY_X, 8, 4, x_prev).start()
-        arrived(RELAY_Y)
-        kv_copy(RELAY_Y, 2, 5, x_next).start()
+        for half in range(2):
+            arrived(4, half)
+            kv_copy(4, 6, 3, y_pair, half).start()
+            share(4, half)
+            arrived(RELAY_X, half)
+            kv_copy(RELAY_X, 8, 4, x_prev, half).start()
+            arrived(RELAY_Y, half)
+            kv_copy(RELAY_Y, 2, 5, x_next, half).start()
 
     @pl.when(y_hi == 1)
     def _():
-        arrived(8)
-        kv_copy(8, 6, 3, y_pair).start()
-        kv_copy(0, 4, 2, x_next).start()
-        share(8)
-        arrived(2)
-        share(2)
+        for half in range(2):
+            arrived(8, half)
+            kv_copy(8, 6, 3, y_pair, half).start()
+            kv_copy(0, 4, 2, x_next, half).start()
+            share(8, half)
+            arrived(2, half)
+            share(2, half)
 
     early = (4 + 4 * y_hi, 2 * y_hi + (1 - y_hi) * (3 + 2 * core))
     late = (
@@ -258,19 +265,17 @@
 
     @pl.when(y_hi == 0)
     def _():
-        arrived(2)
-        share(2)
-        arrived(6)
-        share(6)
-        arrived(8)
-        share(8)
+        for half in range(2):
+            for slot in (2, 6, 8):
+                arrived(slot, half)
+                share(slot, half)
 
     @pl.when(y_hi == 1)
     def _():
-        arrived(4)
-        share(4)
-        arrived(6)
-        share(6)
+        for half in range(2):
+            for slot in (4, 6):
+                arrived(slot, half)
+                share(slot, half)
         arrived(1)
 
     for slot in late[:3]:
@@ -437,13 +442,15 @@
         z_copy(6, n).wait_recv()
         two_ref[:, (NY + n) * PCOLS : (NY + n + 1) * PCOLS] = mate_in[n]
 
-    for send in (0, 1, 2, 3, 6, 7, 8, 9):
-        kv_copy(0, 0, send, sibling).wait_send()
+    for half in range(2):
+        for send in (0, 1, 2, 3, 6, 7, 8, 9):
+            kv_copy(0, 0, send, sibling, half).wait_send()
 
     @pl.when(y_hi == 0)
     def _():
-        for send in (4, 5):
-            kv_copy(0, 0, send, sibling).wait_send()
+        for half in range(2):
+            for send in (4, 5):
+                kv_copy(0, 0, send, sibling, half).wait_send()
 
     for n in range(NZ):
         for kind in range(7):
@@ -485,8 +492,8 @@
             pltpu.VMEM((3, NY, 64, PCOLS), bf16),
             pltpu.VMEM((2, NY, 32, PCOLS), bf16),
             pltpu.VMEM((2, NY, 64, PCOLS), bf16),
-            pltpu.SemaphoreType.DMA((10,)),
-            pltpu.SemaphoreType.DMA((SLOTS + 2,)),
+            pltpu.SemaphoreType.DMA((10, 2)),
+            pltpu.SemaphoreType.DMA((SLOTS + 2, 2)),
             pltpu.SemaphoreType.DMA((7, NZ)),
             pltpu.SemaphoreType.DMA((7, NZ)),
             pltpu.SemaphoreType.DMA((10, NY)),
@@ -498,7 +505,7 @@
             pltpu.SemaphoreType.DMA((4,)),
         ],
         compiler_params=pltpu.CompilerParams(
-            collective_id=0, has_side_effects=True, vmem_limit_bytes=56 * 2**20
+            collective_id=0, has_side_effects=True, vmem_limit_bytes=52 * 2**20
         ),
         cost_estimate=pl.CostEstimate(
             flops=14 * 10**9, bytes_accessed=10 * 2**20, transcendentals=19 * 10**6

time: 61.3 us -> 63.2 us (1.031)
  local copies, waits for them, and re-layouts: 0 us -> 2.49 us
  other arithmetic: 2.12 us -> 0.92 us
    unnamed x0 -> x6, local copies, waits for them, and re-layouts: none -> 2.49 us
    convert_element_type x1, other arithmetic: 2.12 us -> 0.92 us  [on_device(): return (one.astype(f32) + two.astype(f32)).astype(bf16)]
where the time goes in v6:
time: 63.2 us; the launch traced here: 63 us
  Pallas kernels  59.6 us (94%)
  local copies, waits for them, and re-layouts  2.49 us (4%)
  other arithmetic  0.92 us (1%)
    pallas_call x1, Pallas kernels, on_device(): pl.pallas_call(kernel, name='attend_project', out_shape=[jax.ShapeDtypeSt...  59.6 us
    unnamed x6, local copies, waits for them, and re-layouts  2.49 us

profile of v6, /device:TPU:1, one launch (start us, length us, event | category | flops | bytes accessed | tf_op | source)
XLA Modules:
  0.0 63.0 jit_solution(15914755748471516097)
XLA Ops:
  0.0 0.0 copy-start
  0.0 0.9 %copy-done = bf16[512,128]{1,0:T(8,128)(2,1)S(1)} copy-done((bf16[512,128]{1,0:T(8,128)(2,1)S(1)}, bf16[512,128]{1,0:T(8,128)(2,1)}, u32[]{:S(2)}) %copy-start) | copy-done | bytes 131096
  0.9 0.0 copy-start.1
  0.9 0.9 %copy-done.1 = bf16[512,128]{1,0:T(8,128)(2,1)S(1)} copy-done((bf16[512,128]{1,0:T(8,128)(2,1)S(1)}, bf16[512,128]{1,0:T(8,128)(2,1)}, u32[]{:S(2)}) %copy-start.1) | copy-done | bytes 131096
  1.8 0.0 copy-start.2
  1.8 0.7 %copy-done.2 = s32[512]{0:T(512)S(1)} copy-done((s32[512]{0:T(512)S(1)}, s32[512]{0:T(512)}, u32[]{:S(2)}) %copy-start.2) | copy-done | bytes 2072
  2.5 59.6 %attend_project.1 = (bf16[64,4096]{1,0:T(8,128)(2,1)S(1)}, bf16[64,4096]{1,0:T(8,128)(2,1)S(1)}) custom-call(bf16[512,1024]{1,0:T(8,128)(2,1)} %q_hbm.1, bf16[512,128]{1,0:T(8,128)(2,1)S(1)} %copy-done, bf16[512,128]{1,0:T(8,128)(2,1)S(1)} %copy-done.1, s32[4,128]{1,0:T(4,128)S(1)} %bitcast.1, bf16[1024,4096]{1,0:T(8,128)(2,1)} %w_hbm.1), custom_call_target="tpu_custom_call" | custom-call | flops 14000000000 | bytes 10485760 | tf_op jit(solution)/shard_map/attend_project/pallas_call | solution.py:465
  62.1 0.9 %add_convert_fusion = bf16[64,4096]{1,0:T(8,128)(2,1)} fusion(bf16[64,4096]{1,0:T(8,128)(2,1)S(1)} %get-tuple-element.8, bf16[64,4096]{1,0:T(8,128)(2,1)S(1)} %get-tuple-element.7), kind=kLoop, calls=%fused_computation | loop fusion | flops 1048576 | bytes 1572864 | tf_op jit(solution)/shard_map/convert_element_type | solution.py:514
Async XLA Ops:
  0.0 0.9 %copy-start = (bf16[512,128]{1,0:T(8,128)(2,1)S(1)}, bf16[512,128]{1,0:T(8,128)(2,1)}, u32[]{:S(2)}) copy-start(bf16[512,128]{1,0:T(8,128)(2,1)} %k_hbm.1) | copy-start | bytes 393220
  0.9 0.9 %copy-start.1 = (bf16[512,128]{1,0:T(8,128)(2,1)S(1)}, bf16[512,128]{1,0:T(8,128)(2,1)}, u32[]{:S(2)}) copy-start(bf16[512,128]{1,0:T(8,128)(2,1)} %v_hbm.1) | copy-start | bytes 393220
  1.8 0.7 %copy-start.2 = (s32[512]{0:T(512)S(1)}, s32[512]{0:T(512)}, u32[]{:S(2)}) copy-start(s32[512]{0:T(512)} %param.8) | copy-start | bytes 6148

commit v7 on v5

--- a/solution.py
+++ b/solution.py
@@ -455,6 +455,10 @@
 
 def on_device(queries, key_states, value_states, doc_ids, out_weight):
     vmem = pl.BlockSpec(memory_space=pltpu.VMEM)
+    in_hbm = [
+        pltpu.with_memory_space_constraint(a, pltpu.HBM)
+        for a in (queries, key_states, value_states, doc_ids.reshape(4, 128), out_weight)
+    ]
     one, two = pl.pallas_call(
         kernel,
         name="attend_project",
@@ -498,12 +502,12 @@
             pltpu.SemaphoreType.DMA((4,)),
         ],
         compiler_params=pltpu.CompilerParams(
-            collective_id=0, has_side_effects=True, vmem_limit_bytes=56 * 2**20
+            collective_id=0, has_side_effects=True, vmem_limit_bytes=52 * 2**20
         ),
         cost_estimate=pl.CostEstimate(
             flops=14 * 10**9, bytes_accessed=10 * 2**20, transcendentals=19 * 10**6
         ),
-    )(queries, key_states, value_states, doc_ids.reshape(4, 128), out_weight)
+    )(*in_hbm)
     return (one.astype(f32) + two.astype(f32)).astype(bf16)
 
 

time: 61.3 us -> 59 us (0.962)
  other arithmetic: 2.12 us -> 0.92 us
  Pallas kernels: 59 us -> 58 us
    convert_element_type x1, other arithmetic: 2.12 us -> 0.92 us  [on_device(): return (one.astype(f32) + two.astype(f32)).astype(bf16)]
    pallas_call x1, Pallas kernels: 59 us -> 58 us  [on_device(): pl.pallas_call(kernel, name='attend_project', out_shape=[jax.ShapeDtypeSt...]
where the time goes in v7:
time: 59 us; the launch traced here: 58.9 us
  Pallas kernels  58 us (98%)
  other arithmetic  0.92 us (2%)
    pallas_call x1, Pallas kernels, on_device(): pl.pallas_call(kernel, name='attend_project', out_shape=[jax.ShapeDtypeSt...  58 us

profile of v7, /device:TPU:1, one launch (start us, length us, event | category | flops | bytes accessed | tf_op | source)
XLA Modules:
  0.0 58.9 jit_solution(11445149047685071534)
XLA Ops:
  0.0 58.0 %attend_project.1 = (bf16[64,4096]{1,0:T(8,128)(2,1)S(1)}, bf16[64,4096]{1,0:T(8,128)(2,1)S(1)}) custom-call(bf16[512,1024]{1,0:T(8,128)(2,1)} %q_hbm.1, bf16[512,128]{1,0:T(8,128)(2,1)} %k_hbm.1, bf16[512,128]{1,0:T(8,128)(2,1)} %v_hbm.1, s32[4,128]{1,0:T(4,128)} %bitcast.1, bf16[1024,4096]{1,0:T(8,128)(2,1)} %w_hbm.1), custom_call_target="tpu_custom_call" | custom-call | flops 14000000000 | bytes 10485760 | tf_op jit(solution)/shard_map/attend_project/pallas_call | solution.py:462
  58.0 0.9 %add_convert_fusion = bf16[64,4096]{1,0:T(8,128)(2,1)} fusion(bf16[64,4096]{1,0:T(8,128)(2,1)S(1)} %get-tuple-element.8, bf16[64,4096]{1,0:T(8,128)(2,1)S(1)} %get-tuple-element.7), kind=kLoop, calls=%fused_computation | loop fusion | flops 1048576 | bytes 1572864 | tf_op jit(solution)/shard_map/convert_element_type | solution.py:511

commit v8 on v7

--- a/solution.py
+++ b/solution.py
@@ -136,7 +136,15 @@
 
     for r in range(4):
         kf[0, r * 128 : (r + 1) * 128, :] = jnp.where(id_columns(0, r) == lane, 1.0, 0.0).astype(bf16)
-    for t in range(4):
+    for sub in range(2):
+        for half in range(2):
+            rows = pl.ds(pl.multiple_of(firsts[0][half] + 32 * sub, 32), 32)
+            marks = kf[0, rows, :]
+            for head in range(8):
+                unit, place = 2 * sub + head // 4, head % 4 * 64 + half * 32
+                qx[unit, place : place + 32, 0:128] = q_ref[rows, head * 128 : (head + 1) * 128]
+                qx[unit, place : place + 32, 128:256] = marks
+    for t in range(1, 4):
         for half in range(2):
             rows = pl.ds(pl.multiple_of(firsts[t][half], 64), 64)
             marks = kf[0, rows, :]
@@ -162,6 +170,9 @@
             low_first = ((z + low) % 4) * 64
             high_first = ((z + high) % 4) * 64 + 192
             q_index = lane_q + jnp.where(lane_q < 64, low_first, high_first)
+            lane_0 = lane_q % 64
+            q_index_0 = lane_0 + jnp.where(lane_0 < 32, low_first, high_first + 32) + unit // 2 * 32
+            q_index = jnp.where(t == 0, q_index_0, q_index)
             s = jnp.where(key_index <= q_index, s, FAR)
         s_ref[i * TOK : (i + 1) * TOK, :] = s
         return jnp.max(s.reshape(TOK // 8, 8, 256), axis=0)
@@ -201,20 +212,21 @@
 
     def run(first, count, slots, diagonal=False):
         stage(first, None, slots, pair[0], None, diagonal)
+        steps = min(4, count)
 
         def body(i, carry):
-            for e in range(4):
-                now = first + 4 * i + e
+            for e in range(steps):
+                now = first + steps * i + e
                 ahead = now + 1
-                if e == 3:
-                    ahead = None if count == 4 else jnp.minimum(ahead, first + count - 1)
+                if e == steps - 1:
+                    ahead = None if count == steps else jnp.minimum(ahead, first + count - 1)
                 stage(ahead, now, slots, pair[(e + 1) % 2], pair[e % 2], diagonal)
             return carry
 
-        if count == 4:
+        if count == steps:
             body(0, 0)
         else:
-            lax.fori_loop(0, count // 4, body, 0)
+            lax.fori_loop(0, count // steps, body, 0)
 
     run(0, UNITS, (0,), True)
 
@@ -303,13 +315,15 @@
     def z_copy(kind, n):
         low, high = pl.ds(0, 64), pl.ds(64, 64)
         src, dst, peer = (
-            (part_z.at[0, n, low], a_z.at[n], z_next),
-            (part_z.at[0, n, high], b_z.at[n], z_prev),
+            (part_z.at[0, n, pl.ds(0, 32)], a_z.at[n, pl.ds(0, 32)], z_next),
+            (part_z.at[0, n, pl.ds(64, 32)], b_z.at[n, pl.ds(0, 32)], z_prev),
             (part_z.at[1, n, high], up_z.at[n, high], z_next),
             (part_z.at[2, n, low], up_z.at[n, low], z_next),
             (part_z.at[1, n, low], down_z.at[n, low], z_prev),
             (part_z.at[2, n, high], down_z.at[n, high], z_prev),
             (mate_out.at[n], mate_in.at[n], y_mate),
+            (part_z.at[0, n, pl.ds(32, 32)], a_z.at[n, pl.ds(32, 32)], z_next),
+            (part_z.at[0, n, pl.ds(96, 32)], b_z.at[n, pl.ds(32, 32)], z_prev),
         )[kind]
         return pltpu.make_async_remote_copy(
             src_ref=src, dst_ref=dst, send_sem=z_send.at[kind, n], recv_sem=z_recv.at[kind, n],
@@ -328,7 +342,11 @@
 
     def y_copy(kind, n):
         place = kind
-        if kind < 4:
+        if kind == 0 or kind == 10:
+            sub = kind // 10 * 32
+            rows = pl.ds(pl.multiple_of(64 - y_lo * 64 + sub, 32), 32)
+            src, dst, peer = part_y.at[0, n, rows], met_y.at[0, n, pl.ds(sub, 32)], y_mate
+        elif kind < 4:
             src, dst, peer = part_y.at[kind, n, theirs], met_y.at[kind, n], y_mate
         elif kind < 6:
             src = sum_y.at[0, n, pl.ds(32 * (kind - 4), 32)]
@@ -346,6 +364,8 @@
     def meet(t):
         for n in range(NY):
             y_copy(t, n).wait_recv()
+            if t == 0:
+                y_copy(10, n).wait_recv()
             sum_y[t, n] = (part_y[t, n, mine].astype(f32) + met_y[t, n].astype(f32)).astype(bf16)
             for kind in ((4, 5), (6,), (8,))[t]:
                 y_copy(kind, n).start()
@@ -353,9 +373,11 @@
     def add_far_z():
         for n in range(NZ):
             z_copy(0, n).wait_recv()
+            z_copy(7, n).wait_recv()
             part_z[2, n, 0:64] = (part_z[2, n, 0:64].astype(f32) + a_z[n].astype(f32)).astype(bf16)
             z_copy(3, n).start()
             z_copy(1, n).wait_recv()
+            z_copy(8, n).wait_recv()
             part_z[2, n, 64:128] = (part_z[2, n, 64:128].astype(f32) + b_z[n].astype(f32)).astype(bf16)
             z_copy(5, n).start()
 
@@ -370,13 +392,40 @@
                 ).astype(bf16)
                 y_copy(5 + 2 * t, n).start()
 
-    for t in range(4):
-        if t == 0:
-            run(0, 4, late[:3])
+    for sub in range(2):
+        if sub == 0:
+            run(0, 2, late[:3])
             arrive_last()
-            run(0, 4, late[3:])
+            run(0, 2, late[3:])
         else:
-            run(t * 4, 4, late)
+            run(2, 2, late)
+        for g in range(2):
+            state = acc[2 * sub + g]
+            rows = state[0:128] / state[128:129]
+            for j in range(2):
+                two_heads = rows[:, j * 128 : (j + 1) * 128].T.astype(bf16)
+                for i in range(2):
+                    head = 4 * g + 2 * j + i
+                    att[0:64, head * 128 : (head + 1) * 128] = two_heads[i * 64 : (i + 1) * 64]
+
+        for n in range(NY + NZ):
+            piece = jnp.dot(
+                att[0:64], w[:, n * PCOLS : (n + 1) * PCOLS], preferred_element_type=f32
+            ).astype(bf16)
+            into, i = (part_y, n) if n < NY else (part_z, n - NY)
+            for half in range(2):
+                place = half * 64 + sub * 32
+                into[0, i, place : place + 32] = piece[half * 32 : (half + 1) * 32]
+            if n == NY - 1:
+                for i in range(NY):
+                    y_copy((0, 10)[sub], i).start()
+            if n == NY + 1 or n == NY + 3:
+                for i in (n - NY - 1, n - NY):
+                    for kind in ((0, 1), (7, 8))[sub]:
+                        z_copy(kind, i).start()
+
+    for t in range(1, 4):
+        run(t * 4, 4, late)
         for g in range(4):
             state = acc[t * 4 + g]
             rows = state[0:128] / state[128:129]
@@ -397,10 +446,9 @@
                     y_copy(t, i).start()
             if n == NY + 1 or n == NY + 3:
                 for i in (n - NY - 1, n - NY):
-                    for kind in ((0, 1), (2, 4), (), ())[t]:
+                    for kind in ((), (2, 4), (), ())[t]:
                         z_copy(kind, i).start()
-        if t > 0:
-            meet(t - 1)
+        meet(t - 1)
         if t == 2:
             add_far_z()
 
@@ -446,10 +494,10 @@
             kv_copy(0, 0, send, sibling).wait_send()
 
     for n in range(NZ):
-        for kind in range(7):
+        for kind in range(9):
             z_copy(kind, n).wait_send()
     for n in range(NY):
-        for kind in range(10):
+        for kind in range(11):
             y_copy(kind, n).wait_send()
 
 
@@ -491,10 +539,10 @@
             pltpu.VMEM((2, NY, 64, PCOLS), bf16),
             pltpu.SemaphoreType.DMA((10,)),
             pltpu.SemaphoreType.DMA((SLOTS + 2,)),
-            pltpu.SemaphoreType.DMA((7, NZ)),
-            pltpu.SemaphoreType.DMA((7, NZ)),
-            pltpu.SemaphoreType.DMA((10, NY)),
-            pltpu.SemaphoreType.DMA((10, NY)),
+            pltpu.SemaphoreType.DMA((9, NZ)),
+            pltpu.SemaphoreType.DMA((9, NZ)),
+            pltpu.SemaphoreType.DMA((11, NY)),
+            pltpu.SemaphoreType.DMA((11, NY)),
             pltpu.SemaphoreType.DMA,
             pltpu.VMEM((TOK, 1024), bf16),
             pltpu.VMEM((TOK, 128), bf16),

time: 59 us -> 62.9 us (1.066)
  Pallas kernels: 58 us -> 61.9 us
    pallas_call x1, Pallas kernels: 58 us -> 61.9 us  [on_device(): pl.pallas_call(kernel, name='attend_project', out_shape=[jax.ShapeDtypeSt...]
where the time goes in v8:
time: 62.9 us; the launch traced here: 62.8 us
  Pallas kernels  61.9 us (98%)
  other arithmetic  0.92 us (1%)
    pallas_call x1, Pallas kernels, on_device(): pl.pallas_call(kernel, name='attend_project', out_shape=[jax.ShapeDtypeSt...  61.9 us

profile of v8, /device:TPU:1, one launch (start us, length us, event | category | flops | bytes accessed | tf_op | source)
XLA Modules:
  0.0 62.8 jit_solution(16531845395592521950)
XLA Ops:
  0.0 61.9 %attend_project.1 = (bf16[64,4096]{1,0:T(8,128)(2,1)S(1)}, bf16[64,4096]{1,0:T(8,128)(2,1)S(1)}) custom-call(bf16[512,1024]{1,0:T(8,128)(2,1)} %q_hbm.1, bf16[512,128]{1,0:T(8,128)(2,1)} %k_hbm.1, bf16[512,128]{1,0:T(8,128)(2,1)} %v_hbm.1, s32[4,128]{1,0:T(4,128)} %bitcast.1, bf16[1024,4096]{1,0:T(8,128)(2,1)} %w_hbm.1), custom_call_target="tpu_custom_call" | custom-call | flops 14000000000 | bytes 10485760 | tf_op jit(solution)/shard_map/attend_project/pallas_call | solution.py:510
  61.9 0.9 %add_convert_fusion = bf16[64,4096]{1,0:T(8,128)(2,1)} fusion(bf16[64,4096]{1,0:T(8,128)(2,1)S(1)} %get-tuple-element.8, bf16[64,4096]{1,0:T(8,128)(2,1)S(1)} %get-tuple-element.7), kind=kLoop, calls=%fused_computation | loop fusion | flops 1048576 | bytes 1572864 | tf_op jit(solution)/shard_map/convert_element_type | solution.py:559

commit v9 on v7

--- a/solution.py
+++ b/solution.py
@@ -14,8 +14,8 @@
 RELAY_X, RELAY_Y = 9, 10
 UNITS = 16
 D_OUT = 4096
-PCOLS = 512
-NY, NZ = 4, 4
+PCOLS = 1024
+NY, NZ = 2, 2
 EXP_SCALE = DH**-0.5 * 1.4426950408889634
 FAR = -1e30
 MESH = pl.DeviceIdType.MESH
@@ -395,7 +395,7 @@
             if n == NY - 1:
                 for i in range(NY):
                     y_copy(t, i).start()
-            if n == NY + 1 or n == NY + 3:
+            if n == NY + 1:
                 for i in (n - NY - 1, n - NY):
                     for kind in ((0, 1), (2, 4), (), ())[t]:
                         z_copy(kind, i).start()

time: 59 us -> 59 us (level)
  no operation moved by 1% of the time
where the time goes in v9:
time: 59 us; the launch traced here: 58.6 us
  Pallas kernels  57.6 us (98%)
  other arithmetic  0.92 us (2%)
    pallas_call x1, Pallas kernels, on_device(): pl.pallas_call(kernel, name='attend_project', out_shape=[jax.ShapeDtypeSt...  57.6 us

profile of v9, /device:TPU:1, one launch (start us, length us, event | category | flops | bytes accessed | tf_op | source)
XLA Modules:
  0.0 58.6 jit_solution(15593978072821194199)
XLA Ops:
  0.0 57.6 %attend_project.1 = (bf16[64,4096]{1,0:T(8,128)(2,1)S(1)}, bf16[64,4096]{1,0:T(8,128)(2,1)S(1)}) custom-call(bf16[512,1024]{1,0:T(8,128)(2,1)} %q_hbm.1, bf16[512,128]{1,0:T(8,128)(2,1)} %k_hbm.1, bf16[512,128]{1,0:T(8,128)(2,1)} %v_hbm.1, s32[4,128]{1,0:T(4,128)} %bitcast.1, bf16[1024,4096]{1,0:T(8,128)(2,1)} %w_hbm.1), custom_call_target="tpu_custom_call" | custom-call | flops 14000000000 | bytes 10485760 | tf_op jit(solution)/shard_map/attend_project/pallas_call | solution.py:462
  57.6 0.9 %add_convert_fusion = bf16[64,4096]{1,0:T(8,128)(2,1)} fusion(bf16[64,4096]{1,0:T(8,128)(2,1)S(1)} %get-tuple-element.8, bf16[64,4096]{1,0:T(8,128)(2,1)S(1)} %get-tuple-element.7), kind=kLoop, calls=%fused_computation | loop fusion | flops 1048576 | bytes 1572864 | tf_op jit(solution)/shard_map/convert_element_type | solution.py:511
